TPU v7x, 32 devices: a whole 2x2x4 slice. The times are simulated.
32 devices in a mesh: section: 2 (over x), dp: 4 (over y, core), mp: 4 (over z).
Axes of the slice: x: 2, y: 2, z: 4, core: 2. Of those that a mesh axis runs over, the one named last changes fastest.
Arguments:
- memory: bfloat16 [4, 256, 2048], P('dp', None, ('section', 'mp')), may hold values from -18 to 18
- key_weight: bfloat16 [2, 2048, 2048], P('section', None, 'mp'), may hold values from -1 to 1
- value_weight: bfloat16 [2, 2048, 2048], P('section', None, 'mp'), may hold values from -0.125 to 0.125
- queries: bfloat16 [2, 4, 256, 2048], P('section', 'dp', None, 'mp'), may hold values from -1024 to 1024
- cotangent: bfloat16 [2, 4, 256, 2048], P('section', 'dp', None, 'mp'), may hold values from -6 to 6
- target_lengths: int32 [4], P('dp'), may hold values from 64 to 256, as said below
Outputs:
- context: bfloat16 [2, 4, 256, 2048], P('section', 'dp', None, 'mp')
- mem_grad: float32 [4, 256, 2048], P('dp', None, ('section', 'mp'))
Inputs may be any that keep to these rules, and one draw needn't show every extreme that they name: `target_lengths`: valid positions of a sequence come first; the last sequence is full.
All inputs are finite; a program needn't handle non-finite values.
Results may differ from a plain program's by a relative error of at most 0.013.
The roundings to bfloat16 on the way count: a program that leaves them out, or rounds other values in their place, can miss the bound.
Values may be sent and summed in bfloat16 or wider, within the bound.
A program may use at most 64 MiB of HBM per device.

v0:
```python
import jax
import jax.numpy as jnp
from jax import lax
from jax.sharding import PartitionSpec as P

HEAD_DIM = 256


def on_device(memory, key_weight, value_weight, queries, cotangent, target_lengths):
    width = key_weight.shape[2]
    head_count = width // HEAD_DIM
    seq_rows = queries.shape[2]
    score_scale = HEAD_DIM ** (-0.5)
    mem_block = memory[0]
    mem_rows = mem_block.shape[0]
    full_memory = lax.all_gather(mem_block, ("section", "mp"), axis=1, tiled=True)
    token_total = lax.psum(target_lengths.astype(jnp.float32), "dp")
    slot_total = float(lax.axis_size("dp") * target_lengths.shape[0] * seq_rows)
    loss_weight = slot_total / token_total[0]
    valid = (jnp.arange(seq_rows, dtype=jnp.int32) < target_lengths[0]).astype(jnp.float32)
    layer_index = 0
    key_rows = jnp.dot(
        full_memory, key_weight[layer_index], preferred_element_type=jnp.float32
    ).astype(jnp.bfloat16)
    value_rows = jnp.dot(
        full_memory, value_weight[layer_index], preferred_element_type=jnp.float32
    ).astype(jnp.bfloat16)
    key_heads = key_rows.reshape(mem_rows, head_count, HEAD_DIM)
    value_heads = value_rows.reshape(mem_rows, head_count, HEAD_DIM)
    query_heads = queries[layer_index, 0].reshape(seq_rows, head_count, HEAD_DIM)
    scores = (
        jnp.einsum("thd,shd->hts", query_heads, key_heads, preferred_element_type=jnp.float32)
        * score_scale
    )
    attention = jax.nn.softmax(scores, axis=-1)
    attention_low = attention.astype(jnp.bfloat16)
    context = jnp.einsum(
        "hts,shd->thd", attention_low, value_heads, preferred_element_type=jnp.float32
    )
    context = (context * valid[:, None, None]).astype(jnp.bfloat16)
    contexts = [context.reshape(seq_rows, width)]
    weighted = cotangent[layer_index, 0].astype(jnp.float32) * (valid * loss_weight)[:, None]
    weighted = weighted.astype(jnp.bfloat16).reshape(seq_rows, head_count, HEAD_DIM)
    value_grad = jnp.einsum(
        "hts,thd->shd", attention_low, weighted, preferred_element_type=jnp.float32
    )
    value_grads = [value_grad.astype(jnp.bfloat16).reshape(mem_rows, width)]
    prob_grad = jnp.einsum(
        "thd,shd->hts", weighted, value_heads, preferred_element_type=jnp.float32
    )
    row_dot = jnp.sum(attention * prob_grad, axis=-1, keepdims=True)
    score_grad = (attention * (prob_grad - row_dot) * score_scale).astype(jnp.bfloat16)
    key_grad = jnp.einsum(
        "hts,thd->shd", score_grad, query_heads, preferred_element_type=jnp.float32
    )
    key_grads = [key_grad.astype(jnp.bfloat16).reshape(mem_rows, width)]
    contract_last = (((1,), (1,)), ((), ()))
    layer_index = 0
    key_part = key_weight[layer_index]
    value_part = value_weight[layer_index]
    running = lax.dot_general(
        key_part, key_grads[layer_index], contract_last, preferred_element_type=jnp.float32
    )
    running = running + lax.dot_general(
        value_part, value_grads[layer_index], contract_last, preferred_element_type=jnp.float32
    )
    section_part = lax.psum_scatter(
        running.astype(jnp.bfloat16), "section", scatter_dimension=0, tiled=True
    )
    own_part = lax.psum_scatter(section_part, "mp", scatter_dimension=0, tiled=True).astype(
        jnp.float32
    )
    own_grad = own_part.T
    context_out = jnp.stack(contexts, axis=0)[:, None]
    return (context_out, own_grad[None])


def solution(mesh):
    return jax.shard_map(
        on_device,
        mesh=mesh,
        in_specs=(
            P("dp", None, ("section", "mp")),
            P("section", None, "mp"),
            P("section", None, "mp"),
            P("section", "dp", None, "mp"),
            P("section", "dp", None, "mp"),
            P("dp"),
        ),
        out_specs=(P("section", "dp", None, "mp"), P("dp", None, ("section", "mp"))),
        check_vma=False,
    )
```

profile of v0, /device:TPU:0, one launch (start us, length us, event | category | flops | bytes accessed | tf_op | source)
XLA Modules:
  0.0 117.8 jit_solution(9943838037727948567)
XLA Ops:
  7.2 0.0 all-gather.3.cloned.1.call-start
  7.2 0.7 all-gather.3.cloned.1.call-update
  7.9 0.0 reduce-scatter.3.cloned.1.call-start
  8.6 8.9 %psum.7 = f32[1]{0:T(128)} all-reduce(f32[1]{0:T(128)S(6)} %convert_element_type.66), channel_id=1, replica_groups=mesh['section'=2,'dp'=4,'mp'=4] {'dp'}, use_global_device_ids=true, to_apply=%region_2.0 | all-reduce | flops 1 | bytes 8 | tf_op jit(solution)/shard_map/psum | solution.py:17
  17.5 1.1 copy.25
  18.6 1.1 copy.24
  20.4 32.0 %all-gather.3.cloned.1.call-done = bf16[1,256,2048]{2,1,0:T(8,128)(2,1)} async-done(((bf16[1,256,256]{2,1,0:T(8,128)(2,1)}), bf16[1,256,2048]{2,1,0:T(8,128)(2,1)}) %all-gather.3.cloned.1.call-update) | async-done | bytes 1048592 | tf_op jit(solution)/shard_map/all_gather | solution.py:16
  52.4 1.9 %fusion.23 = bf16[256,512]{1,0:T(8,128)(2,1)S(1)} fusion(bf16[1,2048,512]{2,1,0:T(8,128)(2,1)S(1)} %copy-done, bf16[1,256,2048]{2,1,0:T(8,128)(2,1)} %all-gather.3.cloned.1.call-done), kind=kOutput, calls=%fused_computation.24 | convolution fusion | flops 537001984 | bytes 3407872 | tf_op jit(solution)/shard_map/dot_general | solution.py:22
  54.3 1.1 fusion.59
  55.5 2.6 %fusion.20 = bf16[256,512]{1,0:T(8,128)(2,1)S(1)} fusion(bf16[1,2048,512]{2,1,0:T(8,128)(2,1)} %param.8, bf16[1,256,2048]{2,1,0:T(8,128)(2,1)} %all-gather.3.cloned.1.call-done), kind=kOutput, calls=%fused_computation.23 | convolution fusion | flops 537001984 | bytes 3407872 | tf_op jit(solution)/shard_map/dot_general | solution.py:25
  58.1 0.7 copy-done.2
  58.8 0.2 fusion.34
  59.1 2.2 %convolution_convert_fusion = bf16[2,256,256]{2,1,0:T(8,128)(2,1)} fusion(f32[256,2,256]{0,2,1:T(8,128)S(1)} %bitcast.87, f32[256]{0:T(256)S(1)} %fusion.41, f32[2,256]{1,0:T(2,128)S(1)} %get-tuple-element.4, bf16[256,2,256]{0,2,1:T(8,128)(2,1)S(1)} %bitcast.90, bf16[32,2,8,256]{3,2,1,0:T(8,128)(2,1)} %bitcast.98), kind=kOutput, calls=%fused_computation.25 | convolution fusion | flops 135136000 | bytes 1313792 | tf_op jit(solution)/shard_map/hts,thd->shd/dot_general | solution.py:44
  61.3 1.6 %fusion.19 = bf16[2,256,256]{1,2,0:T(8,128)(2,1)S(1)} fusion(bf16[256,2,256]{0,2,1:T(8,128)(2,1)S(1)} %bitcast.91, f32[2,256,256]{1,2,0:T(8,128)S(1)} %fusion.34, f32[2,256,256]{1,2,0:T(8,128)} %get-tuple-element.5, f32[2,256]{1,0:T(2,128)S(1)} %get-tuple-element.4), kind=kOutput, calls=%fused_computation.22 | convolution fusion | flops 68158208 | bytes 1574912 | tf_op jit(solution)/shard_map/hts,thd->shd/dot_general | solution.py:53
  62.9 0.8 fusion.4
  63.6 0.8 copy-done.1
  64.4 1.8 %fusion.3 = bf16[2048,256]{0,1:T(8,128)(2,1)} fusion(f32[256,2048]{1,0:T(8,128)S(1)} %fusion.4, bf16[256,512]{0,1:T(8,128)(2,1)S(1)} %bitcast.96, bf16[1,2048,512]{2,1,0:T(8,128)(2,1)S(1)} %copy-done.1), kind=kOutput, calls=%fused_computation.4 | convolution fusion | flops 537919488 | bytes 5505024 | tf_op jit(solution)/shard_map/dot_general | solution.py:64
  66.2 0.0 reduce-scatter.3.cloned.1.call-update
  66.2 0.0 reduce-scatter.5.cloned.1.call-start
  66.3 19.3 %reduce-scatter.3.cloned.1.call-done = bf16[1024,256]{0,1:T(8,128)(2,1)} async-done(((bf16[2048,256]{0,1:T(8,128)(2,1)}), bf16[1024,256]{0,1:T(8,128)(2,1)}) %reduce-scatter.3.cloned.1.call-update) | async-done | bytes 524304 | tf_op jit(solution)/shard_map/reduce_scatter | solution.py:67
  85.6 1.5 %fusion.26 = bf16[2,256,256]{2,1,0:T(8,128)(2,1)S(1)} fusion(f32[256]{0:T(256)S(1)} %fusion.42, bf16[32,2,8,256]{3,2,1,0:T(8,128)(2,1)S(1)} %bitcast.95, f32[2,256]{1,0:T(2,128)S(1)} %get-tuple-element.4, bf16[256,2,256]{0,2,1:T(8,128)(2,1)S(1)} %bitcast.92, bf16[32,2,8,256]{3,2,1,0:T(8,128)(2,1)} %bitcast.99), kind=kOutput, calls=%fused_computation.26 | convolution fusion | flops 135004928 | bytes 1051648 | tf_op jit(solution)/shard_map/hts,shd->thd/dot_general | solution.py:37
  87.2 0.8 copy.19
  88.0 21.7 %reduce-scatter.5.cloned.1.call-done = bf16[256,256]{0,1:T(8,128)(2,1)} async-done(((bf16[1024,256]{0,1:T(8,128)(2,1)}), bf16[256,256]{0,1:T(8,128)(2,1)}) %reduce-scatter.5.cloned.1.call-update) | async-done | bytes 131088 | tf_op jit(solution)/shard_map/reduce_scatter | solution.py:70
  109.7 1.6 %convert_bitcast_fusion = f32[1,256,256]{2,1,0:T(8,128)} fusion(bf16[256,256]{0,1:T(8,128)(2,1)} %reduce-scatter.5.cloned.1.call-done), kind=kLoop, calls=%fused_computation.37 | loop fusion | flops 65536 | bytes 393216 | tf_op jit(solution)/shard_map/broadcast_in_dim | solution.py:75
  (13 shorter events, 0.1 us)
Async XLA Ops:
  7.2 45.2 %copy-start = (bf16[1,2048,512]{2,1,0:T(8,128)(2,1)S(1)}, bf16[1,2048,512]{2,1,0:T(8,128)(2,1)}, u32[]{:S(2)}) copy-start(bf16[1,2048,512]{2,1,0:T(8,128)(2,1)} %param.7) | copy-start | bytes 6291460
  7.2 45.2 %all-gather.3.cloned.1.call-start = ((), (), s32[]{:S(2)}) async-start(), calls=%async_computation.4 | async-start | bytes 1179648 | tf_op jit(solution)/shard_map/all_gather | solution.py:16
  7.9 77.7 %reduce-scatter.3.cloned.1.call-start = ((), (), s32[]{:S(2)}) async-start(), calls=%async_computation.2 | async-start | bytes 1572864 | tf_op jit(solution)/shard_map/reduce_scatter | solution.py:67
  54.3 3.8 %copy-start.5 = (bf16[256,512]{1,0:T(8,128)(2,1)}, bf16[256,512]{1,0:T(8,128)(2,1)S(1)}, u32[]{:S(2)}) copy-start(bf16[256,512]{1,0:T(8,128)(2,1)S(1)} %fusion.23) | copy-start | bytes 786436
  58.1 0.7 copy-start.2
  62.9 1.6 %copy-start.1 = (bf16[1,2048,512]{2,1,0:T(8,128)(2,1)S(1)}, bf16[1,2048,512]{2,1,0:T(8,128)(2,1)}, u32[]{:S(2)}) copy-start(bf16[1,2048,512]{2,1,0:T(8,128)(2,1)} %param.8) | copy-start | bytes 6291460
  62.9 1.6 %copy-start.4 = (bf16[2,256,256]{2,1,0:T(8,128)(2,1)S(1)}, bf16[2,256,256]{2,1,0:T(8,128)(2,1)}, u32[]{:S(2)}) copy-start(bf16[2,256,256]{2,1,0:T(8,128)(2,1)} %convolution_convert_fusion) | copy-start | bytes 786436
  64.4 21.2 %copy-start.3 = (bf16[256,512]{1,0:T(8,128)(2,1)S(1)}, bf16[256,512]{1,0:T(8,128)(2,1)}, u32[]{:S(2)}) copy-start(bf16[256,512]{1,0:T(8,128)(2,1)} %copy-done.2) | copy-start | bytes 786436
  66.2 43.4 %reduce-scatter.5.cloned.1.call-start = ((), (), s32[]{:S(2)}) async-start(), calls=%async_computation.3 | async-start | bytes 655360 | tf_op jit(solution)/shard_map/reduce_scatter | solution.py:70
Sparse Core Ops, SparseCore 0:
  10.0 42.3 all-gather.2
  66.3 19.1 reduce-scatter.2
  88.0 21.6 reduce-scatter.4
where the time goes:
time: 118 us
  waiting for transfers between devices  73.7 us (62%)
  between operations  15.2 us (13%)
  matrix products  13.7 us (12%)
  blocking collectives  8.87 us (8%)
  local copies, waits for them, and re-layouts  4.54 us (4%)
  other arithmetic  1.63 us (1%)
    all_gather x1, waiting for transfers between devices, on_device(): lax.all_gather(mem_block, ('section', 'mp'), axis=1, tiled=True)  32 us
    reduce_scatter x1, waiting for transfers between devices, on_device(): lax.psum_scatter(section_part, 'mp', scatter_dimension=0, tiled=True)  21.7 us
    reduce_scatter x1, waiting for transfers between devices, on_device(): lax.psum_scatter(running.astype(jnp.bfloat16), 'section', scatter_dimensi...  19.3 us
    psum x1, blocking collectives, on_device(): token_total = lax.psum(target_lengths.astype(jnp.float32), 'dp')  8.87 us
    dot_general x1, matrix products, on_device(): jnp.dot(full_memory, value_weight[layer_index], preferred_element_type=jn...  2.62 us
    unnamed x13, local copies, waits for them, and re-layouts  2.38 us
  transfers between devices with their start and end apart: 3, of which 3 were waited for; matrix products, arithmetic and copies ran while one was open for 4% of the time, Pallas kernels for 0%

commit v1 on v0

--- a/solution.py
+++ b/solution.py
@@ -1,9 +1,389 @@
+import functools
+
 import jax
 import jax.numpy as jnp
 from jax import lax
+from jax.experimental import pallas as pl
+from jax.experimental.pallas import tpu as pltpu
 from jax.sharding import PartitionSpec as P
 
 HEAD_DIM = 256
+CHUNKS = 2
+MESH = pl.DeviceIdType.MESH
+
+
+def far_to_near(z, n):
+    low, high, order = 0, n - 1, []
+    for _ in range(n):
+        take_low = (z - low) >= (high - z)
+        order.append(jnp.where(take_low, low, high))
+        low, high = jnp.where(take_low, low + 1, low), jnp.where(take_low, high, high - 1)
+    return order
+
+
+def fused_kernel(
+    n, n_dp,
+    len_ref, memory_ref, kw_ref, vw_ref, q_ref, cot_ref,
+    ctx_out, grad_out,
+    kw, vw, q, cot, mem_all, k_acc, v_acc, q_t, w, w_t, ctx, dk_t, dv_t,
+    xs, xr, acc, zs, zr, len_own, len_all,
+    local_sem, ag_own_send, ag_z_send, ag_x_send, ag_recv,
+    rs_x_send, rs_x_recv, rs_z_send, rs_z_recv, len_send, len_recv,
+):
+    x = lax.axis_index("section")
+    z = lax.axis_index("mp")
+    dp = lax.axis_index("dp")
+    other = 1 - x
+    mem_rows, block = memory_ref.shape
+    seq_rows, width = q_ref.shape
+    heads = width // HEAD_DIM
+    score_scale = HEAD_DIM ** (-0.5)
+    part_rows = mem_rows // CHUNKS
+    part_feats = block // CHUNKS
+    far = far_to_near(z, n)
+    near = far[::-1]
+
+    own_slot = x * n + z
+    loads = [
+        pltpu.make_async_copy(src, dst, local_sem.at[i])
+        for i, (src, dst) in enumerate(
+            (
+                (memory_ref, mem_all.at[own_slot]),
+                (q_ref, q),
+                (cot_ref, cot),
+                (kw_ref, kw),
+                (vw_ref, vw),
+            )
+        )
+    ]
+    for load in loads:
+        load.start()
+    length = len_ref[0]
+    len_own[...] = jnp.full(len_own.shape, length.astype(jnp.float32), jnp.float32)
+
+    barrier = pltpu.get_barrier_semaphore()
+    pl.semaphore_signal(barrier, inc=1, device_id={"section": other}, device_id_type=MESH)
+    for r in range(1, n_dp):
+        peer = lax.rem(dp + r, n_dp)
+        pl.semaphore_signal(barrier, inc=1, device_id={"dp": peer}, device_id_type=MESH)
+
+    @pl.when(z > 0)
+    def _():
+        pl.semaphore_signal(barrier, inc=1, device_id={"mp": z - 1}, device_id_type=MESH)
+
+    @pl.when(z < n - 1)
+    def _():
+        pl.semaphore_signal(barrier, inc=1, device_id={"mp": z + 1}, device_id_type=MESH)
+
+    line_peers = jnp.where(z > 0, 1, 0) + jnp.where(z < n - 1, 1, 0)
+    pl.semaphore_wait(barrier, n_dp + line_peers)
+
+    def rows_of(c):
+        return pl.ds(c * part_rows, part_rows)
+
+    def send_block(src, slot, c, send_sem, device_id):
+        return pltpu.make_async_remote_copy(
+            src_ref=src,
+            dst_ref=mem_all.at[slot, rows_of(c)],
+            send_sem=send_sem,
+            recv_sem=ag_recv.at[slot, c],
+            device_id=device_id,
+            device_id_type=MESH,
+        )
+
+    def own_to_left(c):
+        return send_block(memory_ref.at[rows_of(c)], own_slot, c, ag_own_send.at[0, c], {"mp": z - 1})
+
+    def own_to_right(c):
+        return send_block(memory_ref.at[rows_of(c)], own_slot, c, ag_own_send.at[1, c], {"mp": z + 1})
+
+    def to_x(k, c):
+        slot = x * n + near[k]
+        src = memory_ref.at[rows_of(c)] if k == 0 else mem_all.at[slot, rows_of(c)]
+        return send_block(src, slot, c, ag_x_send.at[k, c], {"section": other})
+
+    def relay(k, c):
+        slot = x * n + near[k]
+        dest = jnp.where(near[k] < z, z + 1, z - 1)
+        return send_block(mem_all.at[slot, rows_of(c)], slot, c, ag_z_send.at[k, c], {"mp": dest})
+
+    def relays(k):
+        j = near[k]
+        return ((j < z) & (z < n - 1)) | ((j > z) & (z > 0))
+
+    def arrived(slot, c):
+        send_block(mem_all.at[slot, rows_of(c)], slot, c, ag_x_send.at[0, c], {"section": other}).wait_recv()
+
+    for c in range(CHUNKS):
+
+        @pl.when(z > 0)
+        def _():
+            own_to_left(c).start()
+
+        @pl.when(z < n - 1)
+        def _():
+            own_to_right(c).start()
+
+        to_x(0, c).start()
+
+    def send_length(r):
+        peer = lax.rem(dp + r, n_dp)
+        return pltpu.make_async_remote_copy(
+            src_ref=len_own,
+            dst_ref=len_all.at[dp],
+            send_sem=len_send.at[r],
+            recv_sem=len_recv.at[dp],
+            device_id={"dp": peer},
+            device_id_type=MESH,
+        )
+
+    for r in range(1, n_dp):
+        send_length(r).start()
+
+    def project(slot, first=False):
+        rows = pl.ds(pl.multiple_of(slot * block, block), block)
+        mem_block = mem_all[slot]
+        k_part = jnp.dot(mem_block, kw[rows, :], preferred_element_type=jnp.float32)
+        v_part = jnp.dot(mem_block, vw[rows, :], preferred_element_type=jnp.float32)
+        if first:
+            k_acc[...] = k_part
+            v_acc[...] = v_part
+        else:
+            k_acc[...] += k_part
+            v_acc[...] += v_part
+
+    loads[0].wait()
+    loads[1].wait()
+    q_t[...] = q[...].T
+    loads[2].wait()
+    loads[3].wait()
+    loads[4].wait()
+    project(own_slot, first=True)
+
+    valid = (
+        lax.broadcasted_iota(jnp.int32, (seq_rows, 1), 0) < length
+    ).astype(jnp.float32)
+    for k in range(1, n):
+        for c in range(CHUNKS):
+            arrived(x * n + near[k], c)
+
+            @pl.when(relays(k))
+            def _():
+                relay(k, c).start()
+
+            to_x(k, c).start()
+        if k == 1:
+            total = len_own[...]
+            for r in range(1, n_dp):
+                peer = lax.rem(dp + r, n_dp)
+                pltpu.make_async_remote_copy(
+                    src_ref=len_own,
+                    dst_ref=len_all.at[peer],
+                    send_sem=len_send.at[r],
+                    recv_sem=len_recv.at[peer],
+                    device_id={"dp": peer},
+                    device_id_type=MESH,
+                ).wait_recv()
+                total = total + len_all[peer]
+            loss_weight = (float(n_dp * seq_rows) / total)[0:1, 0:1]
+            weighted = (cot[...].astype(jnp.float32) * (valid * loss_weight)).astype(jnp.bfloat16)
+            w[...] = weighted
+            w_t[...] = weighted.T
+        project(x * n + near[k])
+        if k >= 2:
+            for c in range(CHUNKS):
+                arrived(other * n + near[k - 2], c)
+            project(other * n + near[k - 2])
+    for k in range(max(n - 2, 0), n):
+        for c in range(CHUNKS):
+            arrived(other * n + near[k], c)
+        project(other * n + near[k])
+
+    last = (((1,), (1,)), ((), ()))
+    for h in range(heads):
+        cols = slice(h * HEAD_DIM, (h + 1) * HEAD_DIM)
+        key_h = k_acc[:, cols].astype(jnp.bfloat16)
+        value_h = v_acc[:, cols].astype(jnp.bfloat16)
+        scores = (
+            lax.dot_general(q[:, cols], key_h, last, preferred_element_type=jnp.float32)
+            * score_scale
+        )
+        prob_grad = lax.dot_general(w[:, cols], value_h, last, preferred_element_type=jnp.float32)
+        top = jnp.max(scores, axis=-1, keepdims=True)
+        powers = jnp.exp(scores - top)
+        attention = powers / jnp.sum(powers, axis=-1, keepdims=True)
+        attention_low = attention.astype(jnp.bfloat16)
+        row_dot = jnp.sum(attention * prob_grad, axis=-1, keepdims=True)
+        score_grad = (attention * (prob_grad - row_dot) * score_scale).astype(jnp.bfloat16)
+        dv_t[cols, :] = jnp.dot(
+            w_t[cols, :], attention_low, preferred_element_type=jnp.float32
+        ).astype(jnp.bfloat16)
+        dk_t[cols, :] = jnp.dot(
+            q_t[cols, :], score_grad, preferred_element_type=jnp.float32
+        ).astype(jnp.bfloat16)
+        context = jnp.dot(attention_low, value_h, preferred_element_type=jnp.float32)
+        ctx[:, cols] = (context * valid).astype(jnp.bfloat16)
+    ctx_copy = pltpu.make_async_copy(ctx, ctx_out, local_sem.at[0])
+    ctx_copy.start()
+
+    def feats_of(c):
+        return pl.ds(c * part_feats, part_feats)
+
+    def grad_part(slot, c):
+        rows = pl.ds(pl.multiple_of(slot * block + c * part_feats, part_feats), part_feats)
+        return jnp.dot(
+            kw[rows, :], dk_t[...], preferred_element_type=jnp.float32
+        ) + jnp.dot(vw[rows, :], dv_t[...], preferred_element_type=jnp.float32)
+
+    def sum_to_x(k, c):
+        j = far[k]
+        return pltpu.make_async_remote_copy(
+            src_ref=xs.at[j, feats_of(c)],
+            dst_ref=xr.at[j, feats_of(c)],
+            send_sem=rs_x_send.at[k, c],
+            recv_sem=rs_x_recv.at[j, c],
+            device_id={"section": other},
+            device_id_type=MESH,
+        )
+
+    def sum_along_z(k, c, slot):
+        j = far[k]
+        dest = jnp.where(j > z, z + 1, z - 1)
+        return pltpu.make_async_remote_copy(
+            src_ref=zs.at[j, feats_of(c)],
+            dst_ref=zr.at[slot, feats_of(c)],
+            send_sem=rs_z_send.at[k, c],
+            recv_sem=rs_z_recv.at[slot, c],
+            device_id={"mp": dest},
+            device_id_type=MESH,
+        )
+
+    for k in range(n):
+        for c in range(CHUNKS):
+            xs[far[k], feats_of(c)] = grad_part(other * n + far[k], c).astype(jnp.bfloat16)
+            sum_to_x(k, c).start()
+    for k in range(n):
+        for c in range(CHUNKS):
+            acc[far[k], feats_of(c)] = grad_part(x * n + far[k], c)
+
+    def target_slot(j):
+        return jnp.where((j < z) & (z - 1 == j), n, j)
+
+    for k in range(n - 1):
+        j = far[k]
+        has_source = ((j > z) & (z > 0)) | ((j < z) & (z < n - 1))
+        for c in range(CHUNKS):
+            sum_to_x(k, c).wait_recv()
+            acc[j, feats_of(c)] += xr[j, feats_of(c)].astype(jnp.float32)
+
+            @pl.when(has_source)
+            def _():
+                sum_along_z(k, c, j).wait_recv()
+                acc[j, feats_of(c)] += zr[j, feats_of(c)].astype(jnp.float32)
+
+            zs[j, feats_of(c)] = acc[j, feats_of(c)].astype(jnp.bfloat16)
+            sum_along_z(k, c, target_slot(j)).start()
+
+    for c in range(CHUNKS):
+        sum_to_x(n - 1, c).wait_recv()
+        grad_out[feats_of(c)] = acc[z, feats_of(c)] + xr[z, feats_of(c)].astype(jnp.float32)
+
+        @pl.when(z > 0)
+        def _():
+            sum_along_z(0, c, z).wait_recv()
+            grad_out[feats_of(c)] += zr[z, feats_of(c)].astype(jnp.float32)
+
+        @pl.when(z < n - 1)
+        def _():
+            sum_along_z(0, c, n).wait_recv()
+            grad_out[feats_of(c)] += zr[n, feats_of(c)].astype(jnp.float32)
+
+    for c in range(CHUNKS):
+
+        @pl.when(z > 0)
+        def _():
+            own_to_left(c).wait_send()
+
+        @pl.when(z < n - 1)
+        def _():
+            own_to_right(c).wait_send()
+
+        for k in range(n):
+            to_x(k, c).wait_send()
+            sum_to_x(k, c).wait_send()
+        for k in range(1, n):
+
+            @pl.when(relays(k))
+            def _():
+                relay(k, c).wait_send()
+
+        for k in range(n - 1):
+            sum_along_z(k, c, target_slot(far[k])).wait_send()
+    for r in range(1, n_dp):
+        send_length(r).wait_send()
+    ctx_copy.wait()
+
+
+def fused(n, n_dp, memory, key_weight, value_weight, queries, cotangent, target_lengths):
+    mem_rows, block = memory.shape[1:]
+    feats, width = key_weight.shape[1:]
+    seq_rows = queries.shape[2]
+    low, full = jnp.bfloat16, jnp.float32
+    vmem, sem = pltpu.VMEM, pltpu.SemaphoreType.DMA
+    anywhere = pl.BlockSpec(memory_space=pl.ANY)
+    context, grad = pl.pallas_call(
+        functools.partial(fused_kernel, n, n_dp),
+        out_shape=(
+            jax.ShapeDtypeStruct((seq_rows, width), low),
+            jax.ShapeDtypeStruct((block, mem_rows), full),
+        ),
+        in_specs=[pl.BlockSpec(memory_space=pltpu.SMEM)] + [anywhere] * 5,
+        out_specs=(anywhere, pl.BlockSpec(memory_space=pltpu.VMEM)),
+        scratch_shapes=[
+            vmem((feats, width), low),
+            vmem((feats, width), low),
+            vmem((seq_rows, width), low),
+            vmem((seq_rows, width), low),
+            vmem((2 * n, mem_rows, block), low),
+            vmem((mem_rows, width), full),
+            vmem((mem_rows, width), full),
+            vmem((width, seq_rows), low),
+            vmem((seq_rows, width), low),
+            vmem((width, seq_rows), low),
+            vmem((seq_rows, width), low),
+            vmem((width, mem_rows), low),
+            vmem((width, mem_rows), low),
+            vmem((n, block, mem_rows), low),
+            vmem((n, block, mem_rows), low),
+            vmem((n, block, mem_rows), full),
+            vmem((n, block, mem_rows), low),
+            vmem((n + 1, block, mem_rows), low),
+            vmem((8, 128), full),
+            vmem((n_dp, 8, 128), full),
+            sem((5,)),
+            sem((2, CHUNKS)),
+            sem((n, CHUNKS)),
+            sem((n, CHUNKS)),
+            sem((2 * n, CHUNKS)),
+            sem((n, CHUNKS)),
+            sem((n, CHUNKS)),
+            sem((n, CHUNKS)),
+            sem((n + 1, CHUNKS)),
+            sem((n_dp,)),
+            sem((n_dp,)),
+        ],
+        compiler_params=pltpu.CompilerParams(
+            collective_id=0, has_side_effects=True, vmem_limit_bytes=60 * 1024 * 1024
+        ),
+    )(
+        target_lengths,
+        memory[0],
+        key_weight[0],
+        value_weight[0],
+        queries[0, 0],
+        cotangent[0, 0],
+    )
+    return context[None, None], grad.T[None]
 
 
 def on_device(memory, key_weight, value_weight, queries, cotangent, target_lengths):
@@ -76,8 +456,17 @@
 
 
 def solution(mesh):
+    sections, n, n_dp = mesh.shape["section"], mesh.shape["mp"], mesh.shape["dp"]
+
+    def per_device(memory, key_weight, value_weight, queries, cotangent, target_lengths):
+        args = (memory, key_weight, value_weight, queries, cotangent, target_lengths)
+        part = 128 * CHUNKS
+        if sections == 2 and memory.shape[2] % part == 0 and memory.shape[1] % part == 0:
+            return fused(n, n_dp, *args)
+        return on_device(*args)
+
     return jax.shard_map(
-        on_device,
+        per_device,
         mesh=mesh,
         in_specs=(
             P("dp", None, ("section", "mp")),

time: 118 us -> 44.1 us (0.37)
  waiting for transfers between devices: 73.7 us -> 0 us
  Pallas kernels: 0 us -> 39.1 us
  between operations: 15.2 us -> 1.29 us
  matrix products: 13.7 us -> 0 us
  blocking collectives: 8.87 us -> 0 us
  other arithmetic: 1.63 us -> 0 us
    reduce_scatter x2 -> x0, waiting for transfers between devices: 41 us -> none  [the longest x1 21.7 us: on_device(): lax.psum_scatter(section_part, 'mp', scatter_dimension=0, tiled=True)]
    pallas_call x0 -> x1, Pallas kernels: none -> 39.1 us  [fused(): pl.pallas_call(functools.partial(fused_kernel, n, n_dp), out_shape=(jax.S...]
    all_gather x1 -> x0, waiting for transfers between devices: 32 us -> none  [on_device(): lax.all_gather(mem_block, ('section', 'mp'), axis=1, tiled=True)]
    dot_general x8 -> x0, matrix products: 12.6 us -> none  [the longest x1 2.62 us: on_device(): jnp.dot(full_memory, value_weight[layer_index], preferred_element_type=jn...]
    psum x1 -> x0, blocking collectives: 8.87 us -> none  [on_device(): token_total = lax.psum(target_lengths.astype(jnp.float32), 'dp')]
    broadcast_in_dim x1 -> x0, other arithmetic: 1.62 us -> none  [on_device(): return (context_out, own_grad[None])]
    unnamed x13 -> x2, local copies, waits for them, and re-layouts: 2.38 us -> 3.46 us
  transfers between devices with their start and end apart: 3 -> 0, of which waited for: 3 -> 0; matrix products, arithmetic and copies ran while one was open for 4% -> 0% of each run, Pallas kernels for 0% -> 0%
where the time goes in v1:
time: 44.1 us; the launch traced here: 43.9 us
  Pallas kernels  39.1 us (89%)
  local copies, waits for them, and re-layouts  3.46 us (8%)
  between operations  1.29 us (3%)
    pallas_call x1, Pallas kernels, fused(): pl.pallas_call(functools.partial(fused_kernel, n, n_dp), out_shape=(jax.S...  39.1 us
    unnamed x2, local copies, waits for them, and re-layouts  3.46 us

profile of v1, /device:TPU:0, one launch (start us, length us, event | category | flops | bytes accessed | tf_op | source)
XLA Modules:
  0.0 43.9 jit_solution(6039788781124363025)
XLA Ops:
  1.3 39.1 %shard_map.77 = (bf16[256,512]{1,0:T(8,128)(2,1)}, f32[256,256]{1,0:T(8,128)}) custom-call(s32[1]{0:T(128)S(6)} %copy.10.len_ref, bf16[256,256]{1,0:T(8,128)(2,1)} %bitcast.15, bf16[2048,512]{1,0:T(8,128)(2,1)} %bitcast.9, bf16[2048,512]{1,0:T(8,128)(2,1)} %bitcast.10, bf16[256,512]{1,0:T(8,128)(2,1)} %bitcast.11, bf16[256,512]{1,0:T(8,128)(2,1)} %bitcast.12), custom_call_target="tpu_custom_call" | custom-call | tf_op jit(solution)/shard_map/pallas_call | solution.py:334
  40.4 1.8 %copy.8 = f32[1,256,256]{2,1,0:T(8,128)} copy(f32[1,256,256]{1,2,0:T(8,128)} %bitcast.14) | data formatting | bytes 524288
  42.2 1.7 %copy.11 = bf16[1,1,256,512]{3,2,1,0:T(8,128)(2,1)} copy(bf16[1,1,256,512]{3,2,1,0:T(8,128)(2,1)} %bitcast.13) | data formatting | bytes 524288

commit v2 on v1

--- a/solution.py
+++ b/solution.py
@@ -8,7 +8,8 @@
 from jax.sharding import PartitionSpec as P
 
 HEAD_DIM = 256
-CHUNKS = 2
+CHUNKS = 4
+HALF = CHUNKS // 2
 MESH = pl.DeviceIdType.MESH
 
 
@@ -21,14 +22,27 @@
     return order
 
 
+def finish_kernel(ctx_ref, grad_ref, ctx_out, grad_out, grad, grad_t, sems):
+    ctx_copy = pltpu.make_async_copy(ctx_ref, ctx_out, sems.at[0])
+    load = pltpu.make_async_copy(grad_ref, grad, sems.at[1])
+    load.start()
+    ctx_copy.start()
+    load.wait()
+    grad_t[...] = grad[...].T
+    store = pltpu.make_async_copy(grad_t, grad_out, sems.at[1])
+    store.start()
+    ctx_copy.wait()
+    store.wait()
+
+
 def fused_kernel(
     n, n_dp,
     len_ref, memory_ref, kw_ref, vw_ref, q_ref, cot_ref,
     ctx_out, grad_out,
     kw, vw, q, cot, mem_all, k_acc, v_acc, q_t, w, w_t, ctx, dk_t, dv_t,
-    xs, xr, acc, zs, zr, len_own, len_all,
+    xs, xr, acc, zs, zr, hs, hr, len_own, len_all,
     local_sem, ag_own_send, ag_z_send, ag_x_send, ag_recv,
-    rs_x_send, rs_x_recv, rs_z_send, rs_z_recv, len_send, len_recv,
+    rs_x_send, rs_x_recv, rs_z_send, rs_z_recv, half_ag_send, half_rs_send, half_rs_recv, len_send, len_recv,
 ):
     x = lax.axis_index("section")
     z = lax.axis_index("mp")
@@ -42,6 +56,12 @@
     part_feats = block // CHUNKS
     far = far_to_near(z, n)
     near = far[::-1]
+    pair = z + 1 - 2 * lax.rem(z, 2)
+    seen, other_order = False, []
+    for k in range(n - 1):
+        seen = seen | (near[k] == pair)
+        other_order.append(jnp.where(seen, near[k + 1], near[k]))
+    other_order.append(pair)
 
     own_slot = x * n + z
     loads = [
@@ -140,6 +160,21 @@
     for r in range(1, n_dp):
         send_length(r).start()
 
+    def half_to_pair(c):
+        slot = other * n + z
+        return send_block(
+            mem_all.at[slot, rows_of(c)], slot, c, half_ag_send.at[c], {"mp": pair}
+        )
+
+    def start_to_x(k, c):
+        if c < HALF:
+            to_x(k, c).start()
+        else:
+
+            @pl.when(near[k] != pair)
+            def _():
+                to_x(k, c).start()
+
     def project(slot, first=False):
         rows = pl.ds(pl.multiple_of(slot * block, block), block)
         mem_block = mem_all[slot]
@@ -171,7 +206,7 @@
             def _():
                 relay(k, c).start()
 
-            to_x(k, c).start()
+            start_to_x(k, c)
         if k == 1:
             total = len_own[...]
             for r in range(1, n_dp):
@@ -189,15 +224,18 @@
             weighted = (cot[...].astype(jnp.float32) * (valid * loss_weight)).astype(jnp.bfloat16)
             w[...] = weighted
             w_t[...] = weighted.T
+        if k == n - 1:
+            for c in range(HALF, CHUNKS):
+                half_to_pair(c).start()
         project(x * n + near[k])
         if k >= 2:
             for c in range(CHUNKS):
-                arrived(other * n + near[k - 2], c)
-            project(other * n + near[k - 2])
-    for k in range(max(n - 2, 0), n):
+                arrived(other * n + other_order[k - 2], c)
+            project(other * n + other_order[k - 2])
+    for k in range(n - 2, n):
         for c in range(CHUNKS):
-            arrived(other * n + near[k], c)
-        project(other * n + near[k])
+            arrived(other * n + other_order[k], c)
+        project(other * n + other_order[k])
 
     last = (((1,), (1,)), ((), ()))
     for h in range(heads):
@@ -229,8 +267,13 @@
     def feats_of(c):
         return pl.ds(c * part_feats, part_feats)
 
-    def grad_part(slot, c):
-        rows = pl.ds(pl.multiple_of(slot * block + c * part_feats, part_feats), part_feats)
+    half_feats = block // 2
+
+    def half_of(i):
+        return pl.ds(i * half_feats, half_feats)
+
+    def grad_part(slot, i):
+        rows = pl.ds(pl.multiple_of(slot * block + i * half_feats, half_feats), half_feats)
         return jnp.dot(
             kw[rows, :], dk_t[...], preferred_element_type=jnp.float32
         ) + jnp.dot(vw[rows, :], dv_t[...], preferred_element_type=jnp.float32)
@@ -258,13 +301,44 @@
             device_id_type=MESH,
         )
 
+    def sum_to_pair(c):
+        rows = pl.ds((c - HALF) * part_feats, part_feats)
+        return pltpu.make_async_remote_copy(
+            src_ref=hs.at[rows],
+            dst_ref=hr.at[rows],
+            send_sem=half_rs_send.at[c],
+            recv_sem=half_rs_recv.at[c],
+            device_id={"mp": pair},
+            device_id_type=MESH,
+        )
+
     for k in range(n):
-        for c in range(CHUNKS):
-            xs[far[k], feats_of(c)] = grad_part(other * n + far[k], c).astype(jnp.bfloat16)
+        j = far[k]
+        xs[j, half_of(0)] = grad_part(other * n + j, 0).astype(jnp.bfloat16)
+        for c in range(HALF):
             sum_to_x(k, c).start()
+        if k == n - 1:
+            tail = grad_part(other * n + j, 1)
+            for c in range(HALF, CHUNKS):
+                sum_to_pair(c).wait_recv()
+            xs[j, half_of(1)] = (tail + hr[...].astype(jnp.float32)).astype(jnp.bfloat16)
+            for c in range(HALF, CHUNKS):
+                sum_to_x(k, c).start()
+        else:
+
+            @pl.when(j != pair)
+            def _():
+                xs[j, half_of(1)] = grad_part(other * n + j, 1).astype(jnp.bfloat16)
+                for c in range(HALF, CHUNKS):
+                    sum_to_x(k, c).start()
+
+        if k == 0:
+            hs[...] = grad_part(other * n + pair, 1).astype(jnp.bfloat16)
+            for c in range(HALF, CHUNKS):
+                sum_to_pair(c).start()
     for k in range(n):
-        for c in range(CHUNKS):
-            acc[far[k], feats_of(c)] = grad_part(x * n + far[k], c)
+        for i in range(2):
+            acc[far[k], half_of(i)] = grad_part(x * n + far[k], i)
 
     def target_slot(j):
         return jnp.where((j < z) & (z - 1 == j), n, j)
@@ -273,8 +347,11 @@
         j = far[k]
         has_source = ((j > z) & (z > 0)) | ((j < z) & (z < n - 1))
         for c in range(CHUNKS):
-            sum_to_x(k, c).wait_recv()
-            acc[j, feats_of(c)] += xr[j, feats_of(c)].astype(jnp.float32)
+
+            @pl.when((j != pair) | (c < HALF))
+            def _():
+                sum_to_x(k, c).wait_recv()
+                acc[j, feats_of(c)] += xr[j, feats_of(c)].astype(jnp.float32)
 
             @pl.when(has_source)
             def _():
@@ -309,8 +386,18 @@
             own_to_right(c).wait_send()
 
         for k in range(n):
-            to_x(k, c).wait_send()
-            sum_to_x(k, c).wait_send()
+
+            @pl.when((near[k] != pair) | (c < HALF))
+            def _():
+                to_x(k, c).wait_send()
+
+            @pl.when((far[k] != pair) | (c < HALF))
+            def _():
+                sum_to_x(k, c).wait_send()
+
+        if c >= HALF:
+            half_to_pair(c).wait_send()
+            sum_to_pair(c).wait_send()
         for k in range(1, n):
 
             @pl.when(relays(k))
@@ -358,6 +445,8 @@
             vmem((n, block, mem_rows), full),
             vmem((n, block, mem_rows), low),
             vmem((n + 1, block, mem_rows), low),
+            vmem((block // 2, mem_rows), low),
+            vmem((block // 2, mem_rows), low),
             vmem((8, 128), full),
             vmem((n_dp, 8, 128), full),
             sem((5,)),
@@ -369,6 +458,9 @@
             sem((n, CHUNKS)),
             sem((n, CHUNKS)),
             sem((n + 1, CHUNKS)),
+            sem((CHUNKS,)),
+            sem((CHUNKS,)),
+            sem((CHUNKS,)),
             sem((n_dp,)),
             sem((n_dp,)),
         ],
@@ -383,7 +475,18 @@
         queries[0, 0],
         cotangent[0, 0],
     )
-    return context[None, None], grad.T[None]
+    context, grad = pl.pallas_call(
+        finish_kernel,
+        out_shape=(
+            jax.ShapeDtypeStruct((seq_rows, width), low),
+            jax.ShapeDtypeStruct((mem_rows, block), full),
+        ),
+        in_specs=[anywhere] * 2,
+        out_specs=(anywhere, anywhere),
+        scratch_shapes=[vmem((block, mem_rows), full), vmem((mem_rows, block), full), sem((2,))],
+        compiler_params=pltpu.CompilerParams(vmem_limit_bytes=60 * 1024 * 1024),
+    )(context, grad)
+    return context[None, None], grad[None]
 
 
 def on_device(memory, key_weight, value_weight, queries, cotangent, target_lengths):
@@ -460,8 +563,8 @@
 
     def per_device(memory, key_weight, value_weight, queries, cotangent, target_lengths):
         args = (memory, key_weight, value_weight, queries, cotangent, target_lengths)
-        part = 128 * CHUNKS
-        if sections == 2 and memory.shape[2] % part == 0 and memory.shape[1] % part == 0:
+        mem_rows, block = memory.shape[1:]
+        if sections == 2 and n >= 4 and n % 2 == 0 and mem_rows % 128 == 0 and block % 128 == 0:
             return fused(n, n_dp, *args)
         return on_device(*args)
 

time: 44.1 us -> 50.5 us (1.15)
  Pallas kernels: 39.1 us -> 49.1 us
  local copies, waits for them, and re-layouts: 3.46 us -> 0 us
    pallas_call x0 -> x1, Pallas kernels: none -> 9.06 us  [fused(): pl.pallas_call(finish_kernel, out_shape=(jax.ShapeDtypeStruct((seq_rows,...]
    unnamed x2 -> x0, local copies, waits for them, and re-layouts: 3.46 us -> none
    pallas_call x1, Pallas kernels: 39.1 us -> 40 us  [fused(): pl.pallas_call(functools.partial(fused_kernel, n, n_dp), out_shape=(jax.S...]
where the time goes in v2:
time: 50.5 us; the launch traced here: 50.4 us
  Pallas kernels  49.1 us (97%)
  between operations  1.29 us (3%)
    pallas_call x1, Pallas kernels, fused(): pl.pallas_call(functools.partial(fused_kernel, n, n_dp), out_shape=(jax.S...  40 us
    pallas_call x1, Pallas kernels, fused(): pl.pallas_call(finish_kernel, out_shape=(jax.ShapeDtypeStruct((seq_rows,...  9.06 us

profile of v2, /device:TPU:0, one launch (start us, length us, event | category | flops | bytes accessed | tf_op | source)
XLA Modules:
  0.0 50.4 jit_solution(7125174657092408357)
XLA Ops:
  1.3 40.0 %shard_map.77 = (bf16[256,512]{1,0:T(8,128)(2,1)}, f32[256,256]{1,0:T(8,128)}) custom-call(s32[1]{0:T(128)S(6)} %copy.8.len_ref, bf16[256,256]{1,0:T(8,128)(2,1)} %bitcast.11, bf16[2048,512]{1,0:T(8,128)(2,1)} %bitcast.7, bf16[2048,512]{1,0:T(8,128)(2,1)} %bitcast.8, bf16[256,512]{1,0:T(8,128)(2,1)} %bitcast.9, bf16[256,512]{1,0:T(8,128)(2,1)} %bitcast.10), custom_call_target="tpu_custom_call" | custom-call | tf_op jit(solution)/shard_map/pallas_call | solution.py:421
  41.3 9.1 %shard_map.78 = (bf16[256,512]{1,0:T(8,128)(2,1)}, f32[256,256]{1,0:T(8,128)}) custom-call(bf16[256,512]{1,0:T(8,128)(2,1)} %get-tuple-element.6.ctx_ref, f32[256,256]{1,0:T(8,128)} %get-tuple-element.7.grad_ref), custom_call_target="tpu_custom_call" | custom-call | tf_op jit(solution)/shard_map/pallas_call | solution.py:478

commit v3 on v1

--- a/solution.py
+++ b/solution.py
@@ -19,6 +19,29 @@
         order.append(jnp.where(take_low, low, high))
         low, high = jnp.where(take_low, low + 1, low), jnp.where(take_low, high, high - 1)
     return order
+
+
+def pick(order, at):
+    found = order[0]
+    for i in range(1, len(order)):
+        found = jnp.where(at == i, order[i], found)
+    return found
+
+
+def finish_kernel(ctx_ref, grad_ref, ctx_out, grad_out, ctx, grad, grad_t, sems):
+    grad_load = pltpu.make_async_copy(grad_ref, grad, sems.at[0])
+    ctx_load = pltpu.make_async_copy(ctx_ref, ctx, sems.at[1])
+    grad_load.start()
+    ctx_load.start()
+    grad_load.wait()
+    grad_t[...] = grad[...].T
+    grad_store = pltpu.make_async_copy(grad_t, grad_out, sems.at[2])
+    grad_store.start()
+    ctx_load.wait()
+    ctx_store = pltpu.make_async_copy(ctx, ctx_out, sems.at[3])
+    ctx_store.start()
+    grad_store.wait()
+    ctx_store.wait()
 
 
 def fused_kernel(
@@ -92,15 +115,14 @@
         )
 
     def own_to_left(c):
-        return send_block(memory_ref.at[rows_of(c)], own_slot, c, ag_own_send.at[0, c], {"mp": z - 1})
+        return send_block(mem_all.at[own_slot, rows_of(c)], own_slot, c, ag_own_send.at[0, c], {"mp": z - 1})
 
     def own_to_right(c):
-        return send_block(memory_ref.at[rows_of(c)], own_slot, c, ag_own_send.at[1, c], {"mp": z + 1})
+        return send_block(mem_all.at[own_slot, rows_of(c)], own_slot, c, ag_own_send.at[1, c], {"mp": z + 1})
 
     def to_x(k, c):
         slot = x * n + near[k]
-        src = memory_ref.at[rows_of(c)] if k == 0 else mem_all.at[slot, rows_of(c)]
-        return send_block(src, slot, c, ag_x_send.at[k, c], {"section": other})
+        return send_block(mem_all.at[slot, rows_of(c)], slot, c, ag_x_send.at[k, c], {"section": other})
 
     def relay(k, c):
         slot = x * n + near[k]
@@ -114,6 +136,7 @@
     def arrived(slot, c):
         send_block(mem_all.at[slot, rows_of(c)], slot, c, ag_x_send.at[0, c], {"section": other}).wait_recv()
 
+    loads[0].wait()
     for c in range(CHUNKS):
 
         @pl.when(z > 0)
@@ -140,25 +163,11 @@
     for r in range(1, n_dp):
         send_length(r).start()
 
-    def project(slot, first=False):
-        rows = pl.ds(pl.multiple_of(slot * block, block), block)
-        mem_block = mem_all[slot]
-        k_part = jnp.dot(mem_block, kw[rows, :], preferred_element_type=jnp.float32)
-        v_part = jnp.dot(mem_block, vw[rows, :], preferred_element_type=jnp.float32)
-        if first:
-            k_acc[...] = k_part
-            v_acc[...] = v_part
-        else:
-            k_acc[...] += k_part
-            v_acc[...] += v_part
-
-    loads[0].wait()
     loads[1].wait()
     q_t[...] = q[...].T
+    k_acc[...] = jnp.zeros_like(k_acc)
+    v_acc[...] = jnp.zeros_like(v_acc)
     loads[2].wait()
-    loads[3].wait()
-    loads[4].wait()
-    project(own_slot, first=True)
 
     valid = (
         lax.broadcasted_iota(jnp.int32, (seq_rows, 1), 0) < length
@@ -189,19 +198,29 @@
             weighted = (cot[...].astype(jnp.float32) * (valid * loss_weight)).astype(jnp.bfloat16)
             w[...] = weighted
             w_t[...] = weighted.T
-        project(x * n + near[k])
-        if k >= 2:
+    loads[3].wait()
+    loads[4].wait()
+
+    @pl.loop(0, 2 * n)
+    def _(e):
+        own_row = e < n
+        slot = jnp.where(own_row, x * n, other * n) + pick(near, jnp.where(own_row, e, e - n))
+
+        @pl.when(e >= n)
+        def _():
             for c in range(CHUNKS):
-                arrived(other * n + near[k - 2], c)
-            project(other * n + near[k - 2])
-    for k in range(max(n - 2, 0), n):
-        for c in range(CHUNKS):
-            arrived(other * n + near[k], c)
-        project(other * n + near[k])
+                arrived(slot, c)
+
+        rows = pl.ds(pl.multiple_of(slot * block, block), block)
+        mem_block = mem_all[slot]
+        k_acc[...] += jnp.dot(mem_block, kw[rows, :], preferred_element_type=jnp.float32)
+        v_acc[...] += jnp.dot(mem_block, vw[rows, :], preferred_element_type=jnp.float32)
 
     last = (((1,), (1,)), ((), ()))
-    for h in range(heads):
-        cols = slice(h * HEAD_DIM, (h + 1) * HEAD_DIM)
+
+    @pl.loop(0, heads)
+    def _(h):
+        cols = pl.ds(pl.multiple_of(h * HEAD_DIM, HEAD_DIM), HEAD_DIM)
         key_h = k_acc[:, cols].astype(jnp.bfloat16)
         value_h = v_acc[:, cols].astype(jnp.bfloat16)
         scores = (
@@ -229,73 +248,74 @@
     def feats_of(c):
         return pl.ds(c * part_feats, part_feats)
 
-    def grad_part(slot, c):
-        rows = pl.ds(pl.multiple_of(slot * block + c * part_feats, part_feats), part_feats)
-        return jnp.dot(
-            kw[rows, :], dk_t[...], preferred_element_type=jnp.float32
-        ) + jnp.dot(vw[rows, :], dv_t[...], preferred_element_type=jnp.float32)
-
-    def sum_to_x(k, c):
-        j = far[k]
+    def sum_to_x(j, c):
         return pltpu.make_async_remote_copy(
             src_ref=xs.at[j, feats_of(c)],
             dst_ref=xr.at[j, feats_of(c)],
-            send_sem=rs_x_send.at[k, c],
+            send_sem=rs_x_send.at[j, c],
             recv_sem=rs_x_recv.at[j, c],
             device_id={"section": other},
             device_id_type=MESH,
         )
 
-    def sum_along_z(k, c, slot):
-        j = far[k]
+    def sum_along_z(j, c, slot):
         dest = jnp.where(j > z, z + 1, z - 1)
         return pltpu.make_async_remote_copy(
             src_ref=zs.at[j, feats_of(c)],
             dst_ref=zr.at[slot, feats_of(c)],
-            send_sem=rs_z_send.at[k, c],
+            send_sem=rs_z_send.at[j, c],
             recv_sem=rs_z_recv.at[slot, c],
             device_id={"mp": dest},
             device_id_type=MESH,
         )
 
-    for k in range(n):
-        for c in range(CHUNKS):
-            xs[far[k], feats_of(c)] = grad_part(other * n + far[k], c).astype(jnp.bfloat16)
-            sum_to_x(k, c).start()
-    for k in range(n):
-        for c in range(CHUNKS):
-            acc[far[k], feats_of(c)] = grad_part(x * n + far[k], c)
+    @pl.loop(0, 2 * n)
+    def _(e):
+        sent = e < n
+        j = pick(far, jnp.where(sent, e, e - n))
+        slot = jnp.where(sent, other * n, x * n) + j
+        rows = pl.ds(pl.multiple_of(slot * block, block), block)
+        acc[j] = jnp.dot(
+            kw[rows, :], dk_t[...], preferred_element_type=jnp.float32
+        ) + jnp.dot(vw[rows, :], dv_t[...], preferred_element_type=jnp.float32)
+
+        @pl.when(sent)
+        def _():
+            xs[j] = acc[j].astype(jnp.bfloat16)
+            for c in range(CHUNKS):
+                sum_to_x(j, c).start()
 
     def target_slot(j):
         return jnp.where((j < z) & (z - 1 == j), n, j)
 
-    for k in range(n - 1):
-        j = far[k]
+    @pl.loop(0, n - 1)
+    def _(k):
+        j = pick(far, k)
         has_source = ((j > z) & (z > 0)) | ((j < z) & (z < n - 1))
         for c in range(CHUNKS):
-            sum_to_x(k, c).wait_recv()
+            sum_to_x(j, c).wait_recv()
             acc[j, feats_of(c)] += xr[j, feats_of(c)].astype(jnp.float32)
 
             @pl.when(has_source)
             def _():
-                sum_along_z(k, c, j).wait_recv()
+                sum_along_z(j, c, j).wait_recv()
                 acc[j, feats_of(c)] += zr[j, feats_of(c)].astype(jnp.float32)
 
             zs[j, feats_of(c)] = acc[j, feats_of(c)].astype(jnp.bfloat16)
-            sum_along_z(k, c, target_slot(j)).start()
+            sum_along_z(j, c, target_slot(j)).start()
 
     for c in range(CHUNKS):
-        sum_to_x(n - 1, c).wait_recv()
+        sum_to_x(z, c).wait_recv()
         grad_out[feats_of(c)] = acc[z, feats_of(c)] + xr[z, feats_of(c)].astype(jnp.float32)
 
         @pl.when(z > 0)
         def _():
-            sum_along_z(0, c, z).wait_recv()
+            sum_along_z(far[0], c, z).wait_recv()
             grad_out[feats_of(c)] += zr[z, feats_of(c)].astype(jnp.float32)
 
         @pl.when(z < n - 1)
         def _():
-            sum_along_z(0, c, n).wait_recv()
+            sum_along_z(far[0], c, n).wait_recv()
             grad_out[feats_of(c)] += zr[n, feats_of(c)].astype(jnp.float32)
 
     for c in range(CHUNKS):
@@ -310,7 +330,7 @@
 
         for k in range(n):
             to_x(k, c).wait_send()
-            sum_to_x(k, c).wait_send()
+            sum_to_x(far[k], c).wait_send()
         for k in range(1, n):
 
             @pl.when(relays(k))
@@ -318,7 +338,7 @@
                 relay(k, c).wait_send()
 
         for k in range(n - 1):
-            sum_along_z(k, c, target_slot(far[k])).wait_send()
+            sum_along_z(far[k], c, target_slot(far[k])).wait_send()
     for r in range(1, n_dp):
         send_length(r).wait_send()
     ctx_copy.wait()
@@ -383,7 +403,23 @@
         queries[0, 0],
         cotangent[0, 0],
     )
-    return context[None, None], grad.T[None]
+    context, grad = pl.pallas_call(
+        finish_kernel,
+        out_shape=(
+            jax.ShapeDtypeStruct((seq_rows, width), low),
+            jax.ShapeDtypeStruct((mem_rows, block), full),
+        ),
+        in_specs=[anywhere] * 2,
+        out_specs=(anywhere, anywhere),
+        scratch_shapes=[
+            vmem((seq_rows, width), low),
+            vmem((block, mem_rows), full),
+            vmem((mem_rows, block), full),
+            sem((4,)),
+        ],
+        compiler_params=pltpu.CompilerParams(vmem_limit_bytes=60 * 1024 * 1024),
+    )(context, grad)
+    return context[None, None], grad[None]
 
 
 def on_device(memory, key_weight, value_weight, queries, cotangent, target_lengths):
@@ -460,8 +496,8 @@
 
     def per_device(memory, key_weight, value_weight, queries, cotangent, target_lengths):
         args = (memory, key_weight, value_weight, queries, cotangent, target_lengths)
-        part = 128 * CHUNKS
-        if sections == 2 and memory.shape[2] % part == 0 and memory.shape[1] % part == 0:
+        mem_rows, block = memory.shape[1:]
+        if sections == 2 and n >= 2 and mem_rows % 128 == 0 and block % 128 == 0:
             return fused(n, n_dp, *args)
         return on_device(*args)
 

time: 44.1 us -> 42.8 us (0.971)
  local copies, waits for them, and re-layouts: 3.46 us -> 0 us
  Pallas kernels: 39.1 us -> 41.3 us
    unnamed x2 -> x0, local copies, waits for them, and re-layouts: 3.46 us -> none
    pallas_call x0 -> x1, Pallas kernels: none -> 1.91 us  [fused(): pl.pallas_call(finish_kernel, out_shape=(jax.ShapeDtypeStruct((seq_rows,...]
where the time goes in v3:
time: 42.8 us; the launch traced here: 42.6 us
  Pallas kernels  41.3 us (96%)
  between operations  1.29 us (3%)
    pallas_call x1, Pallas kernels, fused(): pl.pallas_call(functools.partial(fused_kernel, n, n_dp), out_shape=(jax.S...  39.4 us
    pallas_call x1, Pallas kernels, fused(): pl.pallas_call(finish_kernel, out_shape=(jax.ShapeDtypeStruct((seq_rows,...  1.91 us

profile of v3, /device:TPU:0, one launch (start us, length us, event | category | flops | bytes accessed | tf_op | source)
XLA Modules:
  0.0 42.6 jit_solution(9657106165332020280)
XLA Ops:
  1.3 39.4 %shard_map.77 = (bf16[256,512]{1,0:T(8,128)(2,1)}, f32[256,256]{1,0:T(8,128)}) custom-call(s32[1]{0:T(128)S(6)} %copy.8.len_ref, bf16[256,256]{1,0:T(8,128)(2,1)} %bitcast.11, bf16[2048,512]{1,0:T(8,128)(2,1)} %bitcast.7, bf16[2048,512]{1,0:T(8,128)(2,1)} %bitcast.8, bf16[256,512]{1,0:T(8,128)(2,1)} %bitcast.9, bf16[256,512]{1,0:T(8,128)(2,1)} %bitcast.10), custom_call_target="tpu_custom_call" | custom-call | tf_op jit(solution)/shard_map/pallas_call | solution.py:354
  40.7 1.9 %shard_map.78 = (bf16[256,512]{1,0:T(8,128)(2,1)}, f32[256,256]{1,0:T(8,128)}) custom-call(bf16[256,512]{1,0:T(8,128)(2,1)} %get-tuple-element.6.ctx_ref, f32[256,256]{1,0:T(8,128)} %get-tuple-element.7.grad_ref), custom_call_target="tpu_custom_call" | custom-call | tf_op jit(solution)/shard_map/pallas_call | solution.py:406

commit v4 on v3

--- a/solution.py
+++ b/solution.py
@@ -50,7 +50,7 @@
     ctx_out, grad_out,
     kw, vw, q, cot, mem_all, k_acc, v_acc, q_t, w, w_t, ctx, dk_t, dv_t,
     xs, xr, acc, zs, zr, len_own, len_all,
-    local_sem, ag_own_send, ag_z_send, ag_x_send, ag_recv,
+    local_sem, ag_z_send, ag_x_send, ag_recv,
     rs_x_send, rs_x_recv, rs_z_send, rs_z_recv, len_send, len_recv,
 ):
     x = lax.axis_index("section")
@@ -90,16 +90,9 @@
         peer = lax.rem(dp + r, n_dp)
         pl.semaphore_signal(barrier, inc=1, device_id={"dp": peer}, device_id_type=MESH)
 
-    @pl.when(z > 0)
-    def _():
-        pl.semaphore_signal(barrier, inc=1, device_id={"mp": z - 1}, device_id_type=MESH)
-
-    @pl.when(z < n - 1)
-    def _():
-        pl.semaphore_signal(barrier, inc=1, device_id={"mp": z + 1}, device_id_type=MESH)
-
-    line_peers = jnp.where(z > 0, 1, 0) + jnp.where(z < n - 1, 1, 0)
-    pl.semaphore_wait(barrier, n_dp + line_peers)
+    for k in range(1, n):
+        pl.semaphore_signal(barrier, inc=1, device_id={"mp": near[k]}, device_id_type=MESH)
+    pl.semaphore_wait(barrier, n_dp + n - 1)
 
     def rows_of(c):
         return pl.ds(c * part_rows, part_rows)
@@ -114,40 +107,25 @@
             device_id_type=MESH,
         )
 
-    def own_to_left(c):
-        return send_block(mem_all.at[own_slot, rows_of(c)], own_slot, c, ag_own_send.at[0, c], {"mp": z - 1})
-
-    def own_to_right(c):
-        return send_block(mem_all.at[own_slot, rows_of(c)], own_slot, c, ag_own_send.at[1, c], {"mp": z + 1})
+    def to_line(k, c):
+        return send_block(
+            mem_all.at[own_slot, rows_of(c)], own_slot, c, ag_z_send.at[k, c], {"mp": near[k]}
+        )
 
     def to_x(k, c):
         slot = x * n + near[k]
         return send_block(mem_all.at[slot, rows_of(c)], slot, c, ag_x_send.at[k, c], {"section": other})
 
-    def relay(k, c):
-        slot = x * n + near[k]
-        dest = jnp.where(near[k] < z, z + 1, z - 1)
-        return send_block(mem_all.at[slot, rows_of(c)], slot, c, ag_z_send.at[k, c], {"mp": dest})
-
-    def relays(k):
-        j = near[k]
-        return ((j < z) & (z < n - 1)) | ((j > z) & (z > 0))
-
     def arrived(slot, c):
         send_block(mem_all.at[slot, rows_of(c)], slot, c, ag_x_send.at[0, c], {"section": other}).wait_recv()
 
     loads[0].wait()
     for c in range(CHUNKS):
-
-        @pl.when(z > 0)
-        def _():
-            own_to_left(c).start()
-
-        @pl.when(z < n - 1)
-        def _():
-            own_to_right(c).start()
-
+        to_line(1, c).start()
         to_x(0, c).start()
+    for k in range(2, n):
+        for c in range(CHUNKS):
+            to_line(k, c).start()
 
     def send_length(r):
         peer = lax.rem(dp + r, n_dp)
@@ -175,11 +153,6 @@
     for k in range(1, n):
         for c in range(CHUNKS):
             arrived(x * n + near[k], c)
-
-            @pl.when(relays(k))
-            def _():
-                relay(k, c).start()
-
             to_x(k, c).start()
         if k == 1:
             total = len_own[...]
@@ -259,13 +232,12 @@
         )
 
     def sum_along_z(j, c, slot):
-        dest = jnp.where(j > z, z + 1, z - 1)
         return pltpu.make_async_remote_copy(
             src_ref=zs.at[j, feats_of(c)],
             dst_ref=zr.at[slot, feats_of(c)],
             send_sem=rs_z_send.at[j, c],
             recv_sem=rs_z_recv.at[slot, c],
-            device_id={"mp": dest},
+            device_id={"mp": j},
             device_id_type=MESH,
         )
 
@@ -285,60 +257,31 @@
             for c in range(CHUNKS):
                 sum_to_x(j, c).start()
 
-    def target_slot(j):
-        return jnp.where((j < z) & (z - 1 == j), n, j)
-
     @pl.loop(0, n - 1)
     def _(k):
         j = pick(far, k)
-        has_source = ((j > z) & (z > 0)) | ((j < z) & (z < n - 1))
         for c in range(CHUNKS):
             sum_to_x(j, c).wait_recv()
-            acc[j, feats_of(c)] += xr[j, feats_of(c)].astype(jnp.float32)
-
-            @pl.when(has_source)
-            def _():
-                sum_along_z(j, c, j).wait_recv()
-                acc[j, feats_of(c)] += zr[j, feats_of(c)].astype(jnp.float32)
-
-            zs[j, feats_of(c)] = acc[j, feats_of(c)].astype(jnp.bfloat16)
-            sum_along_z(j, c, target_slot(j)).start()
+            zs[j, feats_of(c)] = (
+                acc[j, feats_of(c)] + xr[j, feats_of(c)].astype(jnp.float32)
+            ).astype(jnp.bfloat16)
+            sum_along_z(j, c, z).start()
 
     for c in range(CHUNKS):
         sum_to_x(z, c).wait_recv()
-        grad_out[feats_of(c)] = acc[z, feats_of(c)] + xr[z, feats_of(c)].astype(jnp.float32)
-
-        @pl.when(z > 0)
-        def _():
-            sum_along_z(far[0], c, z).wait_recv()
-            grad_out[feats_of(c)] += zr[z, feats_of(c)].astype(jnp.float32)
-
-        @pl.when(z < n - 1)
-        def _():
-            sum_along_z(far[0], c, n).wait_recv()
-            grad_out[feats_of(c)] += zr[n, feats_of(c)].astype(jnp.float32)
+        total = acc[z, feats_of(c)] + xr[z, feats_of(c)].astype(jnp.float32)
+        for k in range(1, n):
+            sum_along_z(near[k], c, near[k]).wait_recv()
+            total = total + zr[near[k], feats_of(c)].astype(jnp.float32)
+        grad_out[feats_of(c)] = total
 
     for c in range(CHUNKS):
-
-        @pl.when(z > 0)
-        def _():
-            own_to_left(c).wait_send()
-
-        @pl.when(z < n - 1)
-        def _():
-            own_to_right(c).wait_send()
-
         for k in range(n):
             to_x(k, c).wait_send()
             sum_to_x(far[k], c).wait_send()
         for k in range(1, n):
-
-            @pl.when(relays(k))
-            def _():
-                relay(k, c).wait_send()
-
-        for k in range(n - 1):
-            sum_along_z(far[k], c, target_slot(far[k])).wait_send()
+            to_line(k, c).wait_send()
+            sum_along_z(near[k], c, z).wait_send()
     for r in range(1, n_dp):
         send_length(r).wait_send()
     ctx_copy.wait()
@@ -377,18 +320,17 @@
             vmem((n, block, mem_rows), low),
             vmem((n, block, mem_rows), full),
             vmem((n, block, mem_rows), low),
-            vmem((n + 1, block, mem_rows), low),
+            vmem((n, block, mem_rows), low),
             vmem((8, 128), full),
             vmem((n_dp, 8, 128), full),
             sem((5,)),
-            sem((2, CHUNKS)),
             sem((n, CHUNKS)),
             sem((n, CHUNKS)),
             sem((2 * n, CHUNKS)),
             sem((n, CHUNKS)),
             sem((n, CHUNKS)),
             sem((n, CHUNKS)),
-            sem((n + 1, CHUNKS)),
+            sem((n, CHUNKS)),
             sem((n_dp,)),
             sem((n_dp,)),
         ],

time: 42.8 us -> 43.7 us (1.021)
  Pallas kernels: 41.3 us -> 42.2 us
    pallas_call x1, Pallas kernels: 39.4 us -> 40.3 us  [fused(): pl.pallas_call(functools.partial(fused_kernel, n, n_dp), out_shape=(jax.S...]
where the time goes in v4:
time: 43.7 us; the launch traced here: 43.5 us
  Pallas kernels  42.2 us (97%)
  between operations  1.29 us (3%)
    pallas_call x1, Pallas kernels, fused(): pl.pallas_call(functools.partial(fused_kernel, n, n_dp), out_shape=(jax.S...  40.3 us
    pallas_call x1, Pallas kernels, fused(): pl.pallas_call(finish_kernel, out_shape=(jax.ShapeDtypeStruct((seq_rows,...  1.91 us

profile of v4, /device:TPU:0, one launch (start us, length us, event | category | flops | bytes accessed | tf_op | source)
XLA Modules:
  0.0 43.5 jit_solution(7116416484275700386)
XLA Ops:
  1.3 40.3 %shard_map.77 = (bf16[256,512]{1,0:T(8,128)(2,1)}, f32[256,256]{1,0:T(8,128)}) custom-call(s32[1]{0:T(128)S(6)} %copy.8.len_ref, bf16[256,256]{1,0:T(8,128)(2,1)} %bitcast.11, bf16[2048,512]{1,0:T(8,128)(2,1)} %bitcast.7, bf16[2048,512]{1,0:T(8,128)(2,1)} %bitcast.8, bf16[256,512]{1,0:T(8,128)(2,1)} %bitcast.9, bf16[256,512]{1,0:T(8,128)(2,1)} %bitcast.10), custom_call_target="tpu_custom_call" | custom-call | tf_op jit(solution)/shard_map/pallas_call | solution.py:297
  41.6 1.9 %shard_map.78 = (bf16[256,512]{1,0:T(8,128)(2,1)}, f32[256,256]{1,0:T(8,128)}) custom-call(bf16[256,512]{1,0:T(8,128)(2,1)} %get-tuple-element.6.ctx_ref, f32[256,256]{1,0:T(8,128)} %get-tuple-element.7.grad_ref), custom_call_target="tpu_custom_call" | custom-call | tf_op jit(solution)/shard_map/pallas_call | solution.py:348

commit v5 on v3

--- a/solution.py
+++ b/solution.py
@@ -9,6 +9,7 @@
 
 HEAD_DIM = 256
 CHUNKS = 2
+TURN_AT = 2
 MESH = pl.DeviceIdType.MESH
 
 
@@ -51,7 +52,7 @@
     kw, vw, q, cot, mem_all, k_acc, v_acc, q_t, w, w_t, ctx, dk_t, dv_t,
     xs, xr, acc, zs, zr, len_own, len_all,
     local_sem, ag_own_send, ag_z_send, ag_x_send, ag_recv,
-    rs_x_send, rs_x_recv, rs_z_send, rs_z_recv, len_send, len_recv,
+    rs_x_send, rs_x_recv, rs_z_send, rs_z_recv, len_send, len_recv, turn_sem,
 ):
     x = lax.axis_index("section")
     z = lax.axis_index("mp")
@@ -136,18 +137,18 @@
     def arrived(slot, c):
         send_block(mem_all.at[slot, rows_of(c)], slot, c, ag_x_send.at[0, c], {"section": other}).wait_recv()
 
-    loads[0].wait()
-    for c in range(CHUNKS):
-
-        @pl.when(z > 0)
-        def _():
-            own_to_left(c).start()
-
-        @pl.when(z < n - 1)
-        def _():
-            own_to_right(c).start()
-
-        to_x(0, c).start()
+    def send_own():
+        for c in range(CHUNKS):
+
+            @pl.when(z > 0)
+            def _():
+                own_to_left(c).start()
+
+            @pl.when(z < n - 1)
+            def _():
+                own_to_right(c).start()
+
+            to_x(0, c).start()
 
     def send_length(r):
         peer = lax.rem(dp + r, n_dp)
@@ -162,12 +163,24 @@
 
     for r in range(1, n_dp):
         send_length(r).start()
-
+    loads[0].wait()
+
+    paired = n_dp % 2 == 0
+    first = (lax.rem(dp, 2) == 1) if paired else True
+    if paired:
+        pl.when(first)(send_own)
+    else:
+        send_own()
     loads[1].wait()
     q_t[...] = q[...].T
     k_acc[...] = jnp.zeros_like(k_acc)
     v_acc[...] = jnp.zeros_like(v_acc)
-    loads[2].wait()
+    if paired:
+
+        @pl.when(jnp.logical_not(first))
+        def _():
+            pl.semaphore_wait(turn_sem, 1)
+            send_own()
 
     valid = (
         lax.broadcasted_iota(jnp.int32, (seq_rows, 1), 0) < length
@@ -181,23 +194,29 @@
                 relay(k, c).start()
 
             to_x(k, c).start()
-        if k == 1:
-            total = len_own[...]
-            for r in range(1, n_dp):
-                peer = lax.rem(dp + r, n_dp)
-                pltpu.make_async_remote_copy(
-                    src_ref=len_own,
-                    dst_ref=len_all.at[peer],
-                    send_sem=len_send.at[r],
-                    recv_sem=len_recv.at[peer],
-                    device_id={"dp": peer},
-                    device_id_type=MESH,
-                ).wait_recv()
-                total = total + len_all[peer]
-            loss_weight = (float(n_dp * seq_rows) / total)[0:1, 0:1]
-            weighted = (cot[...].astype(jnp.float32) * (valid * loss_weight)).astype(jnp.bfloat16)
-            w[...] = weighted
-            w_t[...] = weighted.T
+        if paired and k == min(TURN_AT, n - 1):
+
+            @pl.when(first)
+            def _():
+                pl.semaphore_signal(turn_sem, inc=1, device_id={"dp": dp - 1}, device_id_type=MESH)
+
+    total = len_own[...]
+    for r in range(1, n_dp):
+        peer = lax.rem(dp + r, n_dp)
+        pltpu.make_async_remote_copy(
+            src_ref=len_own,
+            dst_ref=len_all.at[peer],
+            send_sem=len_send.at[r],
+            recv_sem=len_recv.at[peer],
+            device_id={"dp": peer},
+            device_id_type=MESH,
+        ).wait_recv()
+        total = total + len_all[peer]
+    loss_weight = (float(n_dp * seq_rows) / total)[0:1, 0:1]
+    loads[2].wait()
+    weighted = (cot[...].astype(jnp.float32) * (valid * loss_weight)).astype(jnp.bfloat16)
+    w[...] = weighted
+    w_t[...] = weighted.T
     loads[3].wait()
     loads[4].wait()
 
@@ -230,7 +249,7 @@
         prob_grad = lax.dot_general(w[:, cols], value_h, last, preferred_element_type=jnp.float32)
         top = jnp.max(scores, axis=-1, keepdims=True)
         powers = jnp.exp(scores - top)
-        attention = powers / jnp.sum(powers, axis=-1, keepdims=True)
+        attention = powers * (1.0 / jnp.sum(powers, axis=-1, keepdims=True))
         attention_low = attention.astype(jnp.bfloat16)
         row_dot = jnp.sum(attention * prob_grad, axis=-1, keepdims=True)
         score_grad = (attention * (prob_grad - row_dot) * score_scale).astype(jnp.bfloat16)
@@ -391,6 +410,7 @@
             sem((n + 1, CHUNKS)),
             sem((n_dp,)),
             sem((n_dp,)),
+            pltpu.SemaphoreType.REGULAR,
         ],
         compiler_params=pltpu.CompilerParams(
             collective_id=0, has_side_effects=True, vmem_limit_bytes=60 * 1024 * 1024

time: 42.8 us -> 47.6 us (1.11)
  Pallas kernels: 41.3 us -> 46.2 us
    pallas_call x1, Pallas kernels: 39.4 us -> 44.3 us  [fused(): pl.pallas_call(functools.partial(fused_kernel, n, n_dp), out_shape=(jax.S...]
where the time goes in v5:
time: 47.6 us; the launch traced here: 47.5 us
  Pallas kernels  46.2 us (97%)
  between operations  1.29 us (3%)
    pallas_call x1, Pallas kernels, fused(): pl.pallas_call(functools.partial(fused_kernel, n, n_dp), out_shape=(jax.S...  44.3 us
    pallas_call x1, Pallas kernels, fused(): pl.pallas_call(finish_kernel, out_shape=(jax.ShapeDtypeStruct((seq_rows,...  1.91 us

profile of v5, /device:TPU:0, one launch (start us, length us, event | category | flops | bytes accessed | tf_op | source)
XLA Modules:
  0.0 47.5 jit_solution(16657642691641544105)
XLA Ops:
  1.3 44.3 %shard_map.77 = (bf16[256,512]{1,0:T(8,128)(2,1)}, f32[256,256]{1,0:T(8,128)}) custom-call(s32[1]{0:T(128)S(6)} %copy.8.len_ref, bf16[256,256]{1,0:T(8,128)(2,1)} %bitcast.11, bf16[2048,512]{1,0:T(8,128)(2,1)} %bitcast.7, bf16[2048,512]{1,0:T(8,128)(2,1)} %bitcast.8, bf16[256,512]{1,0:T(8,128)(2,1)} %bitcast.9, bf16[256,512]{1,0:T(8,128)(2,1)} %bitcast.10), custom_call_target="tpu_custom_call" | custom-call | tf_op jit(solution)/shard_map/pallas_call | solution.py:373
  45.6 1.9 %shard_map.78 = (bf16[256,512]{1,0:T(8,128)(2,1)}, f32[256,256]{1,0:T(8,128)}) custom-call(bf16[256,512]{1,0:T(8,128)(2,1)} %get-tuple-element.6.ctx_ref, f32[256,256]{1,0:T(8,128)} %get-tuple-element.7.grad_ref), custom_call_target="tpu_custom_call" | custom-call | tf_op jit(solution)/shard_map/pallas_call | solution.py:426

commit v6 on v5

--- a/solution.py
+++ b/solution.py
@@ -9,7 +9,7 @@
 
 HEAD_DIM = 256
 CHUNKS = 2
-TURN_AT = 2
+REACH = 2
 MESH = pl.DeviceIdType.MESH
 
 
@@ -52,7 +52,7 @@
     kw, vw, q, cot, mem_all, k_acc, v_acc, q_t, w, w_t, ctx, dk_t, dv_t,
     xs, xr, acc, zs, zr, len_own, len_all,
     local_sem, ag_own_send, ag_z_send, ag_x_send, ag_recv,
-    rs_x_send, rs_x_recv, rs_z_send, rs_z_recv, len_send, len_recv, turn_sem,
+    rs_x_send, rs_x_recv, rs_z_send, rs_z_recv, len_send, len_recv,
 ):
     x = lax.axis_index("section")
     z = lax.axis_index("mp")
@@ -91,16 +91,22 @@
         peer = lax.rem(dp + r, n_dp)
         pl.semaphore_signal(barrier, inc=1, device_id={"dp": peer}, device_id_type=MESH)
 
-    @pl.when(z > 0)
-    def _():
-        pl.semaphore_signal(barrier, inc=1, device_id={"mp": z - 1}, device_id_type=MESH)
-
-    @pl.when(z < n - 1)
-    def _():
-        pl.semaphore_signal(barrier, inc=1, device_id={"mp": z + 1}, device_id_type=MESH)
-
-    line_peers = jnp.where(z > 0, 1, 0) + jnp.where(z < n - 1, 1, 0)
+    line_peers = 0
+    for step in range(1, min(REACH, n - 1) + 1):
+
+        @pl.when(z - step >= 0)
+        def _():
+            pl.semaphore_signal(barrier, inc=1, device_id={"mp": z - step}, device_id_type=MESH)
+
+        @pl.when(z + step < n)
+        def _():
+            pl.semaphore_signal(barrier, inc=1, device_id={"mp": z + step}, device_id_type=MESH)
+
+        line_peers += jnp.where(z - step >= 0, 1, 0) + jnp.where(z + step < n, 1, 0)
     pl.semaphore_wait(barrier, n_dp + line_peers)
+
+    def distance(j):
+        return jnp.where(j > z, j - z, z - j)
 
     def rows_of(c):
         return pl.ds(c * part_rows, part_rows)
@@ -115,11 +121,10 @@
             device_id_type=MESH,
         )
 
-    def own_to_left(c):
-        return send_block(mem_all.at[own_slot, rows_of(c)], own_slot, c, ag_own_send.at[0, c], {"mp": z - 1})
-
-    def own_to_right(c):
-        return send_block(mem_all.at[own_slot, rows_of(c)], own_slot, c, ag_own_send.at[1, c], {"mp": z + 1})
+    def to_line(k, c):
+        return send_block(
+            mem_all.at[own_slot, rows_of(c)], own_slot, c, ag_own_send.at[k, c], {"mp": near[k]}
+        )
 
     def to_x(k, c):
         slot = x * n + near[k]
@@ -132,23 +137,13 @@
 
     def relays(k):
         j = near[k]
-        return ((j < z) & (z < n - 1)) | ((j > z) & (z > 0))
+        return (distance(j) >= REACH) & (((j < z) & (z < n - 1)) | ((j > z) & (z > 0)))
 
     def arrived(slot, c):
         send_block(mem_all.at[slot, rows_of(c)], slot, c, ag_x_send.at[0, c], {"section": other}).wait_recv()
 
-    def send_own():
-        for c in range(CHUNKS):
-
-            @pl.when(z > 0)
-            def _():
-                own_to_left(c).start()
-
-            @pl.when(z < n - 1)
-            def _():
-                own_to_right(c).start()
-
-            to_x(0, c).start()
+    def reached(j):
+        return distance(j) <= REACH
 
     def send_length(r):
         peer = lax.rem(dp + r, n_dp)
@@ -165,23 +160,20 @@
         send_length(r).start()
     loads[0].wait()
 
-    paired = n_dp % 2 == 0
-    first = (lax.rem(dp, 2) == 1) if paired else True
-    if paired:
-        pl.when(first)(send_own)
-    else:
-        send_own()
+    for c in range(CHUNKS):
+        to_line(1, c).start()
+        to_x(0, c).start()
+    for k in range(2, n):
+        for c in range(CHUNKS):
+
+            @pl.when(reached(near[k]))
+            def _():
+                to_line(k, c).start()
+
     loads[1].wait()
     q_t[...] = q[...].T
     k_acc[...] = jnp.zeros_like(k_acc)
     v_acc[...] = jnp.zeros_like(v_acc)
-    if paired:
-
-        @pl.when(jnp.logical_not(first))
-        def _():
-            pl.semaphore_wait(turn_sem, 1)
-            send_own()
-
     valid = (
         lax.broadcasted_iota(jnp.int32, (seq_rows, 1), 0) < length
     ).astype(jnp.float32)
@@ -194,11 +186,6 @@
                 relay(k, c).start()
 
             to_x(k, c).start()
-        if paired and k == min(TURN_AT, n - 1):
-
-            @pl.when(first)
-            def _():
-                pl.semaphore_signal(turn_sem, inc=1, device_id={"dp": dp - 1}, device_id_type=MESH)
 
     total = len_own[...]
     for r in range(1, n_dp):
@@ -278,13 +265,14 @@
         )
 
     def sum_along_z(j, c, slot):
-        dest = jnp.where(j > z, z + 1, z - 1)
+        far_off = distance(j) > REACH
+        step = jnp.where(j > z, z + 1, z - 1)
         return pltpu.make_async_remote_copy(
             src_ref=zs.at[j, feats_of(c)],
             dst_ref=zr.at[slot, feats_of(c)],
             send_sem=rs_z_send.at[j, c],
             recv_sem=rs_z_recv.at[slot, c],
-            device_id={"mp": dest},
+            device_id={"mp": jnp.where(far_off, step, j)},
             device_id_type=MESH,
         )
 
@@ -305,20 +293,22 @@
                 sum_to_x(j, c).start()
 
     def target_slot(j):
-        return jnp.where((j < z) & (z - 1 == j), n, j)
+        return jnp.where(distance(j) > REACH, n + j, z)
 
     @pl.loop(0, n - 1)
     def _(k):
         j = pick(far, k)
-        has_source = ((j > z) & (z > 0)) | ((j < z) & (z < n - 1))
+        has_source = (distance(j) >= REACH) & (
+            ((j > z) & (z > 0)) | ((j < z) & (z < n - 1))
+        )
         for c in range(CHUNKS):
             sum_to_x(j, c).wait_recv()
             acc[j, feats_of(c)] += xr[j, feats_of(c)].astype(jnp.float32)
 
             @pl.when(has_source)
             def _():
-                sum_along_z(j, c, j).wait_recv()
-                acc[j, feats_of(c)] += zr[j, feats_of(c)].astype(jnp.float32)
+                sum_along_z(j, c, n + j).wait_recv()
+                acc[j, feats_of(c)] += zr[n + j, feats_of(c)].astype(jnp.float32)
 
             zs[j, feats_of(c)] = acc[j, feats_of(c)].astype(jnp.bfloat16)
             sum_along_z(j, c, target_slot(j)).start()
@@ -327,30 +317,22 @@
         sum_to_x(z, c).wait_recv()
         grad_out[feats_of(c)] = acc[z, feats_of(c)] + xr[z, feats_of(c)].astype(jnp.float32)
 
-        @pl.when(z > 0)
-        def _():
-            sum_along_z(far[0], c, z).wait_recv()
-            grad_out[feats_of(c)] += zr[z, feats_of(c)].astype(jnp.float32)
-
-        @pl.when(z < n - 1)
-        def _():
-            sum_along_z(far[0], c, n).wait_recv()
-            grad_out[feats_of(c)] += zr[n, feats_of(c)].astype(jnp.float32)
+        for k in range(1, n):
+
+            @pl.when(reached(near[k]))
+            def _():
+                sum_along_z(near[k], c, near[k]).wait_recv()
+                grad_out[feats_of(c)] += zr[near[k], feats_of(c)].astype(jnp.float32)
 
     for c in range(CHUNKS):
-
-        @pl.when(z > 0)
-        def _():
-            own_to_left(c).wait_send()
-
-        @pl.when(z < n - 1)
-        def _():
-            own_to_right(c).wait_send()
-
         for k in range(n):
             to_x(k, c).wait_send()
             sum_to_x(far[k], c).wait_send()
         for k in range(1, n):
+
+            @pl.when(reached(near[k]))
+            def _():
+                to_line(k, c).wait_send()
 
             @pl.when(relays(k))
             def _():
@@ -396,21 +378,20 @@
             vmem((n, block, mem_rows), low),
             vmem((n, block, mem_rows), full),
             vmem((n, block, mem_rows), low),
-            vmem((n + 1, block, mem_rows), low),
+            vmem((2 * n, block, mem_rows), low),
             vmem((8, 128), full),
             vmem((n_dp, 8, 128), full),
             sem((5,)),
-            sem((2, CHUNKS)),
+            sem((n, CHUNKS)),
             sem((n, CHUNKS)),
             sem((n, CHUNKS)),
             sem((2 * n, CHUNKS)),
             sem((n, CHUNKS)),
             sem((n, CHUNKS)),
             sem((n, CHUNKS)),
-            sem((n + 1, CHUNKS)),
+            sem((2 * n, CHUNKS)),
             sem((n_dp,)),
             sem((n_dp,)),
-            pltpu.SemaphoreType.REGULAR,
         ],
         compiler_params=pltpu.CompilerParams(
             collective_id=0, has_side_effects=True, vmem_limit_bytes=60 * 1024 * 1024

time: 47.6 us -> 42.2 us (0.89)
  Pallas kernels: 46.2 us -> 40.7 us
    pallas_call x1, Pallas kernels: 44.3 us -> 38.8 us  [fused(): pl.pallas_call(functools.partial(fused_kernel, n, n_dp), out_shape=(jax.S...]
where the time goes in v6:
time: 42.2 us; the launch traced here: 42 us
  Pallas kernels  40.7 us (96%)
  between operations  1.29 us (3%)
    pallas_call x1, Pallas kernels, fused(): pl.pallas_call(functools.partial(fused_kernel, n, n_dp), out_shape=(jax.S...  38.8 us
    pallas_call x1, Pallas kernels, fused(): pl.pallas_call(finish_kernel, out_shape=(jax.ShapeDtypeStruct((seq_rows,...  1.91 us

profile of v6, /device:TPU:0, one launch (start us, length us, event | category | flops | bytes accessed | tf_op | source)
XLA Modules:
  0.0 42.0 jit_solution(13736296244323149297)
XLA Ops:
  1.3 38.8 %shard_map.77 = (bf16[256,512]{1,0:T(8,128)(2,1)}, f32[256,256]{1,0:T(8,128)}) custom-call(s32[1]{0:T(128)S(6)} %copy.8.len_ref, bf16[256,256]{1,0:T(8,128)(2,1)} %bitcast.11, bf16[2048,512]{1,0:T(8,128)(2,1)} %bitcast.7, bf16[2048,512]{1,0:T(8,128)(2,1)} %bitcast.8, bf16[256,512]{1,0:T(8,128)(2,1)} %bitcast.9, bf16[256,512]{1,0:T(8,128)(2,1)} %bitcast.10), custom_call_target="tpu_custom_call" | custom-call | tf_op jit(solution)/shard_map/pallas_call | solution.py:355
  40.1 1.9 %shard_map.78 = (bf16[256,512]{1,0:T(8,128)(2,1)}, f32[256,256]{1,0:T(8,128)}) custom-call(bf16[256,512]{1,0:T(8,128)(2,1)} %get-tuple-element.6.ctx_ref, f32[256,256]{1,0:T(8,128)} %get-tuple-element.7.grad_ref), custom_call_target="tpu_custom_call" | custom-call | tf_op jit(solution)/shard_map/pallas_call | solution.py:407

commit v7 on v6

--- a/solution.py
+++ b/solution.py
@@ -177,50 +177,55 @@
     valid = (
         lax.broadcasted_iota(jnp.int32, (seq_rows, 1), 0) < length
     ).astype(jnp.float32)
-    for k in range(1, n):
-        for c in range(CHUNKS):
-            arrived(x * n + near[k], c)
-
-            @pl.when(relays(k))
-            def _():
-                relay(k, c).start()
-
-            to_x(k, c).start()
-
-    total = len_own[...]
-    for r in range(1, n_dp):
-        peer = lax.rem(dp + r, n_dp)
-        pltpu.make_async_remote_copy(
-            src_ref=len_own,
-            dst_ref=len_all.at[peer],
-            send_sem=len_send.at[r],
-            recv_sem=len_recv.at[peer],
-            device_id={"dp": peer},
-            device_id_type=MESH,
-        ).wait_recv()
-        total = total + len_all[peer]
-    loss_weight = (float(n_dp * seq_rows) / total)[0:1, 0:1]
-    loads[2].wait()
-    weighted = (cot[...].astype(jnp.float32) * (valid * loss_weight)).astype(jnp.bfloat16)
-    w[...] = weighted
-    w_t[...] = weighted.T
-    loads[3].wait()
-    loads[4].wait()
-
-    @pl.loop(0, 2 * n)
-    def _(e):
-        own_row = e < n
-        slot = jnp.where(own_row, x * n, other * n) + pick(near, jnp.where(own_row, e, e - n))
-
-        @pl.when(e >= n)
-        def _():
-            for c in range(CHUNKS):
-                arrived(slot, c)
-
+    def weigh():
+        total = len_own[...]
+        for r in range(1, n_dp):
+            peer = lax.rem(dp + r, n_dp)
+            pltpu.make_async_remote_copy(
+                src_ref=len_own,
+                dst_ref=len_all.at[peer],
+                send_sem=len_send.at[r],
+                recv_sem=len_recv.at[peer],
+                device_id={"dp": peer},
+                device_id_type=MESH,
+            ).wait_recv()
+            total = total + len_all[peer]
+        loss_weight = (float(n_dp * seq_rows) / total)[0:1, 0:1]
+        loads[2].wait()
+        weighted = (cot[...].astype(jnp.float32) * (valid * loss_weight)).astype(jnp.bfloat16)
+        w[...] = weighted
+        w_t[...] = weighted.T
+
+    def project(slot):
         rows = pl.ds(pl.multiple_of(slot * block, block), block)
         mem_block = mem_all[slot]
         k_acc[...] += jnp.dot(mem_block, kw[rows, :], preferred_element_type=jnp.float32)
         v_acc[...] += jnp.dot(mem_block, vw[rows, :], preferred_element_type=jnp.float32)
+
+    for k in range(1, n):
+        for c in range(CHUNKS):
+            arrived(x * n + near[k], c)
+
+            @pl.when(relays(k))
+            def _():
+                relay(k, c).start()
+
+            to_x(k, c).start()
+        if k == 1:
+            loads[3].wait()
+            loads[4].wait()
+        project(x * n + near[k - 1])
+        if k == min(2, n - 1):
+            weigh()
+
+    @pl.loop(0, n + 1)
+    def _(e):
+        @pl.when(e > 0)
+        def _():
+            for c in range(CHUNKS):
+                arrived(other * n + pick(near, e - 1), c)
+
+        project(jnp.where(e == 0, x * n + near[n - 1], other * n + pick(near, e - 1)))
 
     last = (((1,), (1,)), ((), ()))
 
@@ -276,21 +281,18 @@
             device_id_type=MESH,
         )
 
-    @pl.loop(0, 2 * n)
-    def _(e):
-        sent = e < n
-        j = pick(far, jnp.where(sent, e, e - n))
-        slot = jnp.where(sent, other * n, x * n) + j
+    def grad_part(slot):
         rows = pl.ds(pl.multiple_of(slot * block, block), block)
-        acc[j] = jnp.dot(
+        return jnp.dot(
             kw[rows, :], dk_t[...], preferred_element_type=jnp.float32
         ) + jnp.dot(vw[rows, :], dv_t[...], preferred_element_type=jnp.float32)
 
-        @pl.when(sent)
-        def _():
-            xs[j] = acc[j].astype(jnp.bfloat16)
-            for c in range(CHUNKS):
-                sum_to_x(j, c).start()
+    @pl.loop(0, n)
+    def _(k):
+        j = pick(far, k)
+        xs[j] = grad_part(other * n + j).astype(jnp.bfloat16)
+        for c in range(CHUNKS):
+            sum_to_x(j, c).start()
 
     def target_slot(j):
         return jnp.where(distance(j) > REACH, n + j, z)
@@ -298,6 +300,7 @@
     @pl.loop(0, n - 1)
     def _(k):
         j = pick(far, k)
+        acc[j] = grad_part(x * n + j)
         has_source = (distance(j) >= REACH) & (
             ((j > z) & (z > 0)) | ((j < z) & (z < n - 1))
         )
@@ -313,6 +316,7 @@
             zs[j, feats_of(c)] = acc[j, feats_of(c)].astype(jnp.bfloat16)
             sum_along_z(j, c, target_slot(j)).start()
 
+    acc[z] = grad_part(own_slot)
     for c in range(CHUNKS):
         sum_to_x(z, c).wait_recv()
         grad_out[feats_of(c)] = acc[z, feats_of(c)] + xr[z, feats_of(c)].astype(jnp.float32)

time: 42.2 us -> 42.2 us (level)
  no operation moved by 1% of the time
where the time goes in v7:
time: 42.2 us; the launch traced here: 42.1 us
  Pallas kernels  40.8 us (97%)
  between operations  1.29 us (3%)
    pallas_call x1, Pallas kernels, fused(): pl.pallas_call(functools.partial(fused_kernel, n, n_dp), out_shape=(jax.S...  38.9 us
    pallas_call x1, Pallas kernels, fused(): pl.pallas_call(finish_kernel, out_shape=(jax.ShapeDtypeStruct((seq_rows,...  1.91 us

profile of v7, /device:TPU:0, one launch (start us, length us, event | category | flops | bytes accessed | tf_op | source)
XLA Modules:
  0.0 42.1 jit_solution(5456052921202084957)
XLA Ops:
  1.3 38.9 %shard_map.77 = (bf16[256,512]{1,0:T(8,128)(2,1)}, f32[256,256]{1,0:T(8,128)}) custom-call(s32[1]{0:T(128)S(6)} %copy.8.len_ref, bf16[256,256]{1,0:T(8,128)(2,1)} %bitcast.11, bf16[2048,512]{1,0:T(8,128)(2,1)} %bitcast.7, bf16[2048,512]{1,0:T(8,128)(2,1)} %bitcast.8, bf16[256,512]{1,0:T(8,128)(2,1)} %bitcast.9, bf16[256,512]{1,0:T(8,128)(2,1)} %bitcast.10), custom_call_target="tpu_custom_call" | custom-call | tf_op jit(solution)/shard_map/pallas_call | solution.py:359
  40.2 1.9 %shard_map.78 = (bf16[256,512]{1,0:T(8,128)(2,1)}, f32[256,256]{1,0:T(8,128)}) custom-call(bf16[256,512]{1,0:T(8,128)(2,1)} %get-tuple-element.6.ctx_ref, f32[256,256]{1,0:T(8,128)} %get-tuple-element.7.grad_ref), custom_call_target="tpu_custom_call" | custom-call | tf_op jit(solution)/shard_map/pallas_call | solution.py:411

commit v8 on v7

--- a/solution.py
+++ b/solution.py
@@ -49,7 +49,7 @@
     n, n_dp,
     len_ref, memory_ref, kw_ref, vw_ref, q_ref, cot_ref,
     ctx_out, grad_out,
-    kw, vw, q, cot, mem_all, k_acc, v_acc, q_t, w, w_t, ctx, dk_t, dv_t,
+    kw, vw, q, cot, mem_all, k_acc, v_acc, q_t, w_t, ctx, probs, dk_t, dv_t,
     xs, xr, acc, zs, zr, len_own, len_all,
     local_sem, ag_own_send, ag_z_send, ag_x_send, ag_recv,
     rs_x_send, rs_x_recv, rs_z_send, rs_z_recv, len_send, len_recv,
@@ -193,7 +193,6 @@
         loss_weight = (float(n_dp * seq_rows) / total)[0:1, 0:1]
         loads[2].wait()
         weighted = (cot[...].astype(jnp.float32) * (valid * loss_weight)).astype(jnp.bfloat16)
-        w[...] = weighted
         w_t[...] = weighted.T
 
     def project(slot):
@@ -235,26 +234,22 @@
         key_h = k_acc[:, cols].astype(jnp.bfloat16)
         value_h = v_acc[:, cols].astype(jnp.bfloat16)
         scores = (
-            lax.dot_general(q[:, cols], key_h, last, preferred_element_type=jnp.float32)
-            * score_scale
-        )
-        prob_grad = lax.dot_general(w[:, cols], value_h, last, preferred_element_type=jnp.float32)
-        top = jnp.max(scores, axis=-1, keepdims=True)
+            jnp.dot(key_h, q_t[cols, :], preferred_element_type=jnp.float32) * score_scale
+        )
+        prob_grad = jnp.dot(value_h, w_t[cols, :], preferred_element_type=jnp.float32)
+        top = jnp.max(scores, axis=0, keepdims=True)
         powers = jnp.exp(scores - top)
-        attention = powers * (1.0 / jnp.sum(powers, axis=-1, keepdims=True))
+        attention = powers * (1.0 / jnp.sum(powers, axis=0, keepdims=True))
         attention_low = attention.astype(jnp.bfloat16)
-        row_dot = jnp.sum(attention * prob_grad, axis=-1, keepdims=True)
-        score_grad = (attention * (prob_grad - row_dot) * score_scale).astype(jnp.bfloat16)
-        dv_t[cols, :] = jnp.dot(
-            w_t[cols, :], attention_low, preferred_element_type=jnp.float32
+        probs[h] = attention_low
+        column_dot = jnp.sum(attention * prob_grad, axis=0, keepdims=True)
+        score_grad = (attention * (prob_grad - column_dot) * score_scale).astype(jnp.bfloat16)
+        dv_t[cols, :] = lax.dot_general(
+            w_t[cols, :], attention_low, last, preferred_element_type=jnp.float32
         ).astype(jnp.bfloat16)
-        dk_t[cols, :] = jnp.dot(
-            q_t[cols, :], score_grad, preferred_element_type=jnp.float32
+        dk_t[cols, :] = lax.dot_general(
+            q_t[cols, :], score_grad, last, preferred_element_type=jnp.float32
         ).astype(jnp.bfloat16)
-        context = jnp.dot(attention_low, value_h, preferred_element_type=jnp.float32)
-        ctx[:, cols] = (context * valid).astype(jnp.bfloat16)
-    ctx_copy = pltpu.make_async_copy(ctx, ctx_out, local_sem.at[0])
-    ctx_copy.start()
 
     def feats_of(c):
         return pl.ds(c * part_feats, part_feats)
@@ -316,6 +311,19 @@
             zs[j, feats_of(c)] = acc[j, feats_of(c)].astype(jnp.bfloat16)
             sum_along_z(j, c, target_slot(j)).start()
 
+    @pl.loop(0, heads)
+    def _(h):
+        cols = pl.ds(pl.multiple_of(h * HEAD_DIM, HEAD_DIM), HEAD_DIM)
+        context = lax.dot_general(
+            probs[h],
+            v_acc[:, cols].astype(jnp.bfloat16),
+            (((0,), (0,)), ((), ())),
+            preferred_element_type=jnp.float32,
+        )
+        ctx[:, cols] = (context * valid).astype(jnp.bfloat16)
+
+    ctx_copy = pltpu.make_async_copy(ctx, ctx_out, local_sem.at[0])
+    ctx_copy.start()
     acc[z] = grad_part(own_slot)
     for c in range(CHUNKS):
         sum_to_x(z, c).wait_recv()
@@ -373,9 +381,9 @@
             vmem((mem_rows, width), full),
             vmem((mem_rows, width), full),
             vmem((width, seq_rows), low),
-            vmem((seq_rows, width), low),
             vmem((width, seq_rows), low),
             vmem((seq_rows, width), low),
+            vmem((width // HEAD_DIM, mem_rows, seq_rows), low),
             vmem((width, mem_rows), low),
             vmem((width, mem_rows), low),
             vmem((n, block, mem_rows), low),

time: 42.2 us -> 42.1 us (level)
  no operation moved by 1% of the time
where the time goes in v8:
time: 42.1 us; the launch traced here: 41.9 us
  Pallas kernels  40.7 us (97%)
  between operations  1.29 us (3%)
    pallas_call x1, Pallas kernels, fused(): pl.pallas_call(functools.partial(fused_kernel, n, n_dp), out_shape=(jax.S...  38.7 us
    pallas_call x1, Pallas kernels, fused(): pl.pallas_call(finish_kernel, out_shape=(jax.ShapeDtypeStruct((seq_rows,...  1.91 us

profile of v8, /device:TPU:0, one launch (start us, length us, event | category | flops | bytes accessed | tf_op | source)
XLA Modules:
  0.0 41.9 jit_solution(16209000287512919616)
XLA Ops:
  1.3 38.7 %shard_map.77 = (bf16[256,512]{1,0:T(8,128)(2,1)}, f32[256,256]{1,0:T(8,128)}) custom-call(s32[1]{0:T(128)S(6)} %copy.8.len_ref, bf16[256,256]{1,0:T(8,128)(2,1)} %bitcast.11, bf16[2048,512]{1,0:T(8,128)(2,1)} %bitcast.7, bf16[2048,512]{1,0:T(8,128)(2,1)} %bitcast.8, bf16[256,512]{1,0:T(8,128)(2,1)} %bitcast.9, bf16[256,512]{1,0:T(8,128)(2,1)} %bitcast.10), custom_call_target="tpu_custom_call" | custom-call | tf_op jit(solution)/shard_map/pallas_call | solution.py:367
  40.0 1.9 %shard_map.78 = (bf16[256,512]{1,0:T(8,128)(2,1)}, f32[256,256]{1,0:T(8,128)}) custom-call(bf16[256,512]{1,0:T(8,128)(2,1)} %get-tuple-element.6.ctx_ref, f32[256,256]{1,0:T(8,128)} %get-tuple-element.7.grad_ref), custom_call_target="tpu_custom_call" | custom-call | tf_op jit(solution)/shard_map/pallas_call | solution.py:419
